TPU v7x, 128 devices: a whole 4x4x4 slice. The times are simulated.
128 devices in a mesh: grp: 2 (over z_lo), tp: 8 (over y, z_hi), dp: 8 (over x, core).
Axes of the slice: x: 4, y: 4, z: 4 (z_hi: 2, z_lo: 2; z = z_hi * 2 + z_lo), core: 2. Of those that a mesh axis runs over, the one named last changes fastest.
Arguments:
- residual: bfloat16 [2, 512, 4096], P('grp', 'dp'), may hold values from -3 to 3
- norm_gain: bfloat16 [2, 4096], P('grp'), may hold values from 0.29882812 to 3
- w_query: bfloat16 [2, 4096, 4096], P('grp', 'dp', 'tp'), may hold values from -0.09375 to 0.09375
- w_key: bfloat16 [2, 4096, 1024], P('grp', 'dp', 'tp'), may hold values from -0.09375 to 0.09375
- w_value: bfloat16 [2, 4096, 1024], P('grp', 'dp', 'tp'), may hold values from -0.09375 to 0.09375
- w_output: bfloat16 [2, 4096, 4096], P('grp', 'tp', 'dp'), may hold values from -0.375 to 0.375
- doc_lengths: int32 [4], replicated, may hold values from 1 to 256, 512 in all
- coder_weight: bfloat16 [65536, 2, 4096], P(('grp', 'tp', 'dp')), may hold values from -0.0625 to 0.0625
- enc_bias: float32 [65536], P(('grp', 'tp', 'dp')), may hold values from -3 to 3
- dec_bias: float32 [2, 4096], replicated, may hold values from -3 to 3
Outputs:
- grad_weight: bfloat16 [65536, 2, 4096], P(('grp', 'tp', 'dp'))
- grad_enc_bias: float32 [65536], P(('grp', 'tp', 'dp'))
- grad_dec_bias: float32 [2, 4096], replicated
Inputs may be any that keep to these rules, and one draw needn't show every extreme that they name: `doc_lengths`: 4 document lengths that add up to 512, one of them exactly 256.
All inputs are finite; a program needn't handle non-finite values.
Results may differ from a plain program's by a relative error of at most 0.007.
The roundings to bfloat16 on the way count: a program that leaves them out, or rounds other values in their place, can miss the bound.
Values may be sent and summed in bfloat16 or wider, within the bound.
A program may use at most 192 MiB of HBM per device.

v0:
```python
import jax
import jax.numpy as jnp
from jax import lax
from jax.sharding import PartitionSpec as P

HEAD_DIM = 128
TOK_DEV = 64


sparsity = 1.0
rope_base = 500000.0


def doc_layout(doc_lengths, token_index):
    doc_ends = jnp.cumsum(doc_lengths)
    passed = (token_index[:, None] >= doc_ends[None, :]).astype(jnp.int32)
    doc_ids = jnp.sum(passed, axis=1)
    doc_start = jnp.sum(passed * doc_lengths[None, :], axis=1)
    return (doc_ids, token_index - doc_start)


def rotate(values, position):
    half_dim = values.shape[-1] // 2
    inv_freq = rope_base ** (-jnp.arange(half_dim, dtype=jnp.float32) * 2.0 / values.shape[-1])
    angles = position.astype(jnp.float32)[:, None] * inv_freq[None, :]
    cosine = jnp.cos(angles)[:, None, :]
    sine_vals = jnp.sin(angles)[:, None, :]
    low_half = values[..., :half_dim]
    high_half = values[..., half_dim:]
    return jnp.concatenate(
        [low_half * cosine - high_half * sine_vals, high_half * cosine + low_half * sine_vals], -1
    )


def gelu_pair(pre_act):
    normal_cdf = 0.5 * (1.0 + lax.erf(pre_act * 0.7071067811865476))
    density = jnp.exp(-0.5 * pre_act * pre_act) * 0.3989422804014327
    return (pre_act * normal_cdf, normal_cdf + pre_act * density)


def shards(
    residual,
    norm_gain,
    w_query,
    w_key,
    w_value,
    w_output,
    doc_lengths,
    coder_weight,
    enc_bias,
    dec_bias,
):
    dp_count = lax.axis_size("dp")
    tokens_all = dp_count * TOK_DEV
    dp_here = lax.axis_index("dp")
    own_index = dp_here * TOK_DEV + jnp.arange(TOK_DEV, dtype=jnp.int32)
    key_index = jnp.arange(tokens_all, dtype=jnp.int32)
    own_doc, own_pos = doc_layout(doc_lengths, own_index)
    key_doc, key_pos = doc_layout(doc_lengths, key_index)
    inputs = residual[0]
    inputs_wide = inputs.astype(jnp.float32)
    normed = (
        inputs_wide
        * lax.rsqrt(jnp.mean(inputs_wide * inputs_wide, -1, keepdims=True) + 1e-05)
        * norm_gain[0].astype(jnp.float32)
    ).astype(jnp.bfloat16)
    query_cols = w_query.shape[2]
    key_cols = w_key.shape[2]
    moved_rows, moved_normed = (
        lax.all_to_all(inputs, "dp", split_axis=1, concat_axis=0, tiled=True),
        lax.all_to_all(normed, "dp", split_axis=1, concat_axis=0, tiled=True),
    )
    joined = jnp.concatenate([w_query[0], w_key[0], w_value[0]], 1)
    summed = lax.psum_scatter(
        jnp.dot(moved_normed, joined, preferred_element_type=jnp.float32),
        "dp",
        scatter_dimension=0,
        tiled=True,
    )
    query_sum = summed[:, :query_cols]
    keys_sum = summed[:, query_cols : query_cols + key_cols]
    values_sum = summed[:, query_cols + key_cols :]
    heads_here = query_cols // HEAD_DIM
    kv_here = key_cols // HEAD_DIM
    group_size = heads_here // kv_here
    query_rot = (
        rotate(query_sum.reshape(TOK_DEV, heads_here, HEAD_DIM), own_pos)
        .astype(jnp.bfloat16)
        .reshape(TOK_DEV, kv_here, group_size, HEAD_DIM)
    )
    keys_rot = (
        rotate(keys_sum.reshape(TOK_DEV, kv_here, HEAD_DIM), own_pos)
        .astype(jnp.bfloat16)
        .reshape(TOK_DEV, key_cols)
    )
    values_bf = values_sum.astype(jnp.bfloat16)
    all_keys, all_values = (
        lax.all_gather(keys_rot, "dp", axis=0, tiled=True),
        lax.all_gather(values_bf, "dp", axis=0, tiled=True),
    )
    all_keys = all_keys.reshape(tokens_all, kv_here, HEAD_DIM)
    all_values = all_values.reshape(tokens_all, kv_here, HEAD_DIM)
    scores = jnp.einsum(
        "qkgh,skh->kgqs", query_rot, all_keys, preferred_element_type=jnp.float32
    ) * HEAD_DIM ** (-0.5)
    allowed = (own_doc[:, None] == key_doc[None, :]) & (key_index[None, :] <= own_index[:, None])
    exp_terms = jnp.where(allowed, jnp.exp(jnp.where(allowed, scores, 0.0)), 0.0)
    weights = (exp_terms / jnp.sum(exp_terms, -1, keepdims=True)).astype(jnp.bfloat16)
    head_mixed = (
        jnp.einsum("kgqs,skh->qkgh", weights, all_values, preferred_element_type=jnp.float32)
        .astype(jnp.bfloat16)
        .reshape(TOK_DEV, query_cols)
    )
    every_mixed = lax.all_gather(head_mixed, "dp", axis=0, tiled=True)
    partial_value = jnp.dot(every_mixed, w_output[0], preferred_element_type=jnp.float32)
    attn_sum = lax.psum(partial_value, "tp")
    layer_out = (moved_rows.astype(jnp.float32) + attn_sum).astype(jnp.bfloat16)
    col_width = layer_out.shape[1]
    stacked = lax.all_gather(layer_out[None], ("grp", "dp"), axis=0, tiled=True)
    model_rows = (
        stacked.reshape(2, dp_count, tokens_all, col_width)
        .transpose(0, 2, 1, 3)
        .reshape(2, tokens_all, dp_count * col_width)
    )
    model_width = model_rows.shape[2]
    lat_here = coder_weight.shape[0]
    pre_act = (
        jnp.einsum("mtd,lmd->tl", model_rows, coder_weight, preferred_element_type=jnp.float32)
        + enc_bias[None, :]
    )
    latent_act, act_slope = gelu_pair(pre_act)
    act_bf = latent_act.astype(jnp.bfloat16)
    devices = lax.axis_size(("grp", "tp", "dp"))
    own_rows = tokens_all // devices
    coder_flat = coder_weight.reshape(lat_here, 2 * model_width)
    recon_rows = lax.psum_scatter(
        jnp.dot(act_bf, coder_flat, preferred_element_type=jnp.float32),
        ("grp", "tp", "dp"),
        scatter_dimension=0,
        tiled=True,
    )
    row_first = lax.axis_index(("grp", "tp", "dp")) * own_rows
    target = (
        lax.dynamic_slice_in_dim(model_rows, row_first, own_rows, 1)
        .transpose(1, 0, 2)
        .reshape(own_rows, 2 * model_width)
    )
    bias_flat = dec_bias.reshape(1, 2 * model_width)
    row_error = (recon_rows + bias_flat - target.astype(jnp.float32)).astype(jnp.bfloat16)
    errors = lax.all_gather(row_error, ("grp", "tp", "dp"), axis=0, tiled=True).reshape(
        tokens_all, 2, model_width
    )
    weight_wide = coder_weight.astype(jnp.float32)
    dec_norms = jnp.sqrt(jnp.sum(weight_wide * weight_wide, -1) + 1e-06)
    norm_total = jnp.sum(dec_norms, -1)
    act_grad = (
        2.0
        / tokens_all
        * jnp.einsum("tmd,lmd->tl", errors, coder_weight, preferred_element_type=jnp.float32)
        + sparsity / tokens_all * norm_total[None, :]
    )
    pre_grad = act_grad * act_slope
    pre_grad_bf = pre_grad.astype(jnp.bfloat16)
    weight_grad = (
        2.0
        / tokens_all
        * jnp.einsum("tl,tmd->lmd", act_bf, errors, preferred_element_type=jnp.float32)
    )
    weight_grad = weight_grad + jnp.einsum(
        "tl,mtd->lmd", pre_grad_bf, model_rows, preferred_element_type=jnp.float32
    )
    weight_grad = (
        weight_grad
        + sparsity
        / tokens_all
        * jnp.sum(latent_act, 0)[:, None, None]
        * weight_wide
        / dec_norms[:, :, None]
    )
    grad_dec_bias = 2.0 / tokens_all * jnp.sum(errors.astype(jnp.float32), 0)
    return (weight_grad.astype(jnp.bfloat16), jnp.sum(pre_grad, 0), grad_dec_bias)


def solution(mesh):
    return jax.shard_map(
        shards,
        mesh=mesh,
        in_specs=(
            P("grp", "dp", None),
            P("grp", None),
            P("grp", "dp", "tp"),
            P("grp", "dp", "tp"),
            P("grp", "dp", "tp"),
            P("grp", "tp", "dp"),
            P(),
            P(("grp", "tp", "dp"), None, None),
            P(("grp", "tp", "dp")),
            P(),
        ),
        out_specs=(P(("grp", "tp", "dp"), None, None), P(("grp", "tp", "dp")), P()),
        check_vma=False,
    )
```

profile of v0, /device:TPU:1, one launch (start us, length us, event | category | flops | bytes accessed | tf_op | source)
XLA Modules:
  0.0 825.0 jit_solution(13864052696523710652)
XLA Ops:
  7.2 0.0 copy-start
  7.2 0.0 copy-start.3
  7.2 0.0 reduce-scatter.2.cloned.1.call-start
  7.2 1.3 multiply_reduce_fusion
  8.5 0.8 convert_reduce_fusion.1
  9.3 1.2 copy.98
  10.6 0.2 multiply_convert_fusion
  10.7 0.2 copy.78
  10.9 15.0 %all_to_all.29 = bf16[64,8,512]{2,0,1:T(8,128)(2,1)S(1)} all-to-all(bf16[64,8,512]{2,0,1:T(8,128)(2,1)S(1)} %copy.78), channel_id=1, replica_groups=mesh['grp'=2,'tp'=8,'dp'=8] {'dp'}, dimensions={1} | all-to-all | bytes 1048576 | tf_op jit(solution)/shard_map/all_to_all | solution.py:71
  25.9 2.9 fusion.46
  28.8 0.0 reduce-scatter.2.cloned.1.call-update
  28.8 0.0 all-reduce.4.cloned.1.call-start
  28.8 0.0 copy-done.3
  28.9 0.2 reduce-window.8
  29.0 0.1 convert_reduce_fusion.2
  29.1 0.1 fusion.79
  29.2 0.1 fusion.63
  29.3 0.2 multiply_cosine_fusion
  29.5 30.1 %reduce-scatter.2.cloned.1.call-done = f32[64,768]{1,0:T(8,128)} async-done(((f32[512,768]{1,0:T(8,128)}), f32[64,768]{1,0:T(8,128)}) %reduce-scatter.2.cloned.1.call-update) | async-done | bytes 196624 | tf_op jit(solution)/shard_map/reduce_scatter | solution.py:74
  59.6 0.8 slice_bitcast_fusion
  60.4 0.2 fusion.77
  60.6 0.9 slice.33
  61.6 0.1 pad_maximum_fusion
  61.6 16.1 %all_gather.16 = bf16[512,128]{1,0:T(8,128)(2,1)S(1)} all-gather(bf16[64,128]{1,0:T(8,128)(2,1)S(1)} %pad_maximum_fusion), channel_id=1, replica_groups=mesh['grp'=2,'tp'=8,'dp'=8] {'dp'}, dimensions={0}, use_global_device_ids=true | all-gather | bytes 147456 | tf_op jit(solution)/shard_map/all_gather | solution.py:98
  77.7 0.8 slice.50
  78.5 12.7 %all_gather.15 = bf16[512,128]{1,0:T(8,128)(2,1)S(1)} all-gather(bf16[64,128]{1,0:T(8,128)(2,1)S(1)} %slice.50), channel_id=1, replica_groups=mesh['grp'=2,'tp'=8,'dp'=8] {'dp'}, dimensions={0}, use_global_device_ids=true | all-gather | bytes 147456 | tf_op jit(solution)/shard_map/all_gather | solution.py:99
  91.2 0.1 fusion.84
  91.4 0.4 fusion.85
  91.8 0.3 fusion.40
  92.1 0.1 copy.81
  92.2 13.1 %all_gather.17 = bf16[512,512]{1,0:T(8,128)(2,1)S(1)} all-gather(bf16[64,512]{1,0:T(8,128)(2,1)S(1)} %bitcast.107), channel_id=1, replica_groups=mesh['grp'=2,'tp'=8,'dp'=8] {'dp'}, dimensions={0}, use_global_device_ids=true | all-gather | bytes 589824 | tf_op jit(solution)/shard_map/all_gather | solution.py:114
  105.3 0.0 copy-done
  105.3 1.4 fusion.55
  106.7 0.0 all-reduce.4.cloned.1.call-update
  106.7 0.0 all-gather.5.cloned.1.call-start
  106.8 0.2 copy.77
  106.9 12.5 %all_to_all.30 = bf16[64,8,512]{2,0,1:T(8,128)(2,1)S(1)} all-to-all(bf16[64,8,512]{2,0,1:T(8,128)(2,1)S(1)} %copy.77), channel_id=1, replica_groups=mesh['grp'=2,'tp'=8,'dp'=8] {'dp'}, dimensions={1} | all-to-all | bytes 1048576 | tf_op jit(solution)/shard_map/all_to_all | solution.py:70
  119.4 70.6 %all-reduce.4.cloned.1.call-done = f32[512,512]{1,0:T(8,128)} async-done(((f32[512,512]{1,0:T(8,128)}), f32[512,512]{1,0:T(8,128)}) %all-reduce.4.cloned.1.call-update) | async-done | bytes 1048592 | tf_op jit(solution)/shard_map/psum | solution.py:116
  190.0 2.2 fusion.45
  192.2 0.0 all-gather.5.cloned.1.call-update
  192.2 0.5 all-reduce.6.cloned.1.call-start
  192.8 16.2 %copy.100 = bf16[64,8,2,4096]{3,1,2,0:T(8,128)(2,1)} copy(bf16[64,8,2,4096]{3,2,1,0:T(2,128)(2,1)} %bitcast.101) | data formatting | bytes 16777216
  209.0 38.8 %all-gather.5.cloned.1.call-done = bf16[8192,512]{1,0:T(8,128)(2,1)} async-done(((bf16[512,512]{1,0:T(8,128)(2,1)}), bf16[8192,512]{1,0:T(8,128)(2,1)}) %all-gather.5.cloned.1.call-update) | async-done | bytes 8388624 | tf_op jit(solution)/shard_map/all_gather | solution.py:119
  247.7 8.2 copy.97
  256.0 0.0 copy-done.4
  256.0 13.9 %multiply_reduce_fusion.1 = (f32[512]{0:T(512)S(1)}, f32[512,512]{1,0:T(8,128)S(1)}) fusion(f32[512]{0:T(512)S(1)} %copy-done.4, bf16[2,512,4096]{2,1,0:T(8,128)(2,1)} %bitcast.98, bf16[512,2,4096]{2,1,0:T(2,128)(2,1)} %param.17), kind=kOutput, calls=%fused_computation.49 | convolution fusion | flops 4296539648 | bytes 17829888 | tf_op jit(solution)/shard_map/mtd,lmd->tl/dot_general | solution.py:128
  269.9 0.0 slice-done
  269.9 8.1 fusion.83
  278.0 0.0 all-reduce.6.cloned.1.call-update
  278.0 0.0 all-gather.7.cloned.1.call-start
  278.1 0.7 copy-done.2
  278.7 0.9 dynamic-slice_convert_fusion
  279.7 215.6 %all-reduce.6.cloned.1.call-done = f32[512,8192]{1,0:T(8,128)} async-done(((f32[512,8192]{1,0:T(8,128)}), f32[512,8192]{1,0:T(8,128)}) %all-reduce.6.cloned.1.call-update) | async-done | bytes 16777232
  495.3 1.6 fusion.64
  496.9 0.0 all-gather.7.cloned.1.call-update
  496.9 12.2 %fusion = f32[512,2]{0,1:T(2,128)S(1)} fusion(bf16[512,2,4096]{2,1,0:T(2,128)(2,1)} %param.17), kind=kLoop, calls=%fused_computation.2 | loop fusion | flops 12581888 | bytes 8392704 | tf_op jit(solution)/shard_map/reduce_sum | solution.py:154
  509.1 189.1 %all-gather.7.cloned.1.call-done = bf16[128,4,8192]{2,1,0:T(4,128)(2,1)} async-done(((bf16[1,4,8192]{2,1,0:T(4,128)(2,1)}), bf16[128,4,8192]{2,1,0:T(4,128)(2,1)}) %all-gather.7.cloned.1.call-update) | async-done | bytes 8388624 | tf_op jit(solution)/shard_map/all_gather | solution.py:150
  698.3 7.4 convert_reduce_fusion
  705.7 0.6 mul.285
  706.3 15.7 %reshape.265 = bf16[512,2,4096]{2,1,0:T(2,128)(2,1)} reshape(bf16[128,4,8192]{2,1,0:T(4,128)(2,1)} %all-gather.7.cloned.1.call-done) | data formatting | bytes 16777216 | tf_op jit(solution)/shard_map/reshape | solution.py:150
  722.0 28.2 %fusion.86 = (f32[512]{0:T(512)}, bf16[512,512]{1,0:T(8,128)(2,1)S(1)}) fusion(f32[512,512]{1,0:T(8,128)S(1)} %get-tuple-element.36, f32[512]{0:T(512)S(1)} %broadcast_multiply_fusion.2, bf16[512,2,4096]{2,1,0:T(2,128)(2,1)} %param.17, bf16[512,2,4096]{2,1,0:T(2,128)(2,1)} %reshape.265), kind=kOutput, calls=%fused_computation.105 | convolution fusion | flops 4298374656 | bytes 18354176 | tf_op jit(solution)/shard_map/tmd,lmd->tl/dot_general | solution.py:159
  750.3 11.5 %fusion.52 = f32[512,2,4096]{2,0,1:T(8,128)} fusion(bf16[2,512,4096]{2,1,0:T(8,128)(2,1)} %bitcast.100, bf16[512,512]{1,0:T(8,128)(2,1)S(1)} %get-tuple-element.38), kind=kOutput, calls=%fused_computation.42 | convolution fusion | flops 4294967296 | bytes 25690112 | tf_op jit(solution)/shard_map/tl,mtd->lmd/dot_general | solution.py:169
  761.7 40.1 %fusion.3 = bf16[512,2,4096]{2,0,1:T(8,128)(2,1)} fusion(f32[512,2,4096]{2,0,1:T(8,128)} %fusion.52, f32[512,2]{0,1:T(2,128)S(1)} %get-tuple-element.29, f32[512]{0:T(512)S(1)} %broadcast_multiply_fusion.1, bf16[512,2,4096]{2,1,0:T(2,128)(2,1)} %reshape.265, bf16[512,2,4096]{2,1,0:T(2,128)(2,1)} %param.17, f32[512,512]{1,0:T(8,128)S(1)} %get-tuple-element.36), kind=kOutput, calls=%fused_computation.5 | convolution fusion | flops 4325638144 | bytes 42997760 | tf_op jit(solution)/shard_map/tl,tmd->lmd/dot_general | solution.py:167
  801.8 16.4 %copy.90 = bf16[512,2,4096]{2,1,0:T(2,128)(2,1)} copy(bf16[512,2,4096]{2,0,1:T(8,128)(2,1)} %fusion.3) | data formatting | bytes 16777216
  (21 shorter events, 0.2 us)
Async XLA Ops:
  7.2 98.1 %copy-start = (bf16[1,512,512]{2,1,0:T(8,128)(2,1)S(1)}, bf16[1,512,512]{2,1,0:T(8,128)(2,1)}, u32[]{:S(2)}) copy-start(bf16[1,512,512]{2,1,0:T(8,128)(2,1)} %param.15) | copy-start | bytes 1572868
  7.2 21.7 %copy-start.3 = (s32[4]{0:T(128)S(1)}, s32[4]{0:T(128)}, u32[]{:S(2)}) copy-start(s32[4]{0:T(128)} %param.16) | copy-start | bytes 52
  7.2 52.4 %reduce-scatter.2.cloned.1.call-start = ((), (), s32[]{:S(2)}) async-start(), calls=%async_computation.3 | async-start | bytes 1769472 | tf_op jit(solution)/shard_map/reduce_scatter | solution.py:74
  28.8 161.3 %all-reduce.4.cloned.1.call-start = ((), (), s32[]{:S(2)}) async-start(), calls=%async_computation.4 | async-start | bytes 2097152 | tf_op jit(solution)/shard_map/psum | solution.py:116
  106.7 141.0 %all-gather.5.cloned.1.call-start = ((), (), s32[]{:S(2)}) async-start(), calls=%async_computation.5 | async-start | bytes 8912896 | tf_op jit(solution)/shard_map/all_gather | solution.py:119
  192.2 303.1 %all-reduce.6.cloned.1.call-start = ((), (), s32[]{:S(2)}) async-start(), calls=%async_computation.7 | async-start | bytes 33554432
  247.7 8.2 copy-start.4
  247.7 22.1 %slice-start = ((s8[8388608]{0:T(1024)(128)(4,1)}), s8[4194304]{0:T(1024)(128)(4,1)S(1)}, s32[]{:S(2)}) async-start(s8[8388608]{0:T(1024)(128)(4,1)} %bitcast.95), calls=%async_computation.8 | async-start | bytes 8388608
  256.0 13.9 %slice-start.1 = ((s8[8388608]{0:T(1024)(128)(4,1)}), s8[4194304]{0:T(1024)(128)(4,1)S(1)}, s32[]{:S(2)}) async-start(s8[8388608]{0:T(1024)(128)(4,1)} %bitcast.95), calls=%async_computation.9 | async-start | bytes 8388608
  278.0 0.8 copy-start.2
  278.0 420.3 %all-gather.7.cloned.1.call-start = ((), (), s32[]{:S(2)}) async-start(), calls=%async_computation.6 | async-start | bytes 8454144 | tf_op jit(solution)/shard_map/all_gather | solution.py:150
  761.7 56.5 %copy-start.1 = (bf16[1,512,512]{2,1,0:T(8,128)(2,1)S(1)}, bf16[1,512,512]{2,1,0:T(8,128)(2,1)}, u32[]{:S(2)}) copy-start(bf16[1,512,512]{2,1,0:T(8,128)(2,1)} %param.15) | copy-start | bytes 1572868
Sparse Core Ops, SparseCore 0:
  28.9 30.6 reduce-scatter.1
  106.8 83.1 all-reduce.3
  192.4 55.3 all-gather.4
  278.1 217.1 all-reduce.5
  497.1 201.1 all-gather.6
where the time goes:
time: 830 us; the launch traced here: 825 us
  waiting for transfers between devices  544 us (66%)
  matrix products  107 us (13%)
  blocking collectives  69.3 us (8%)
  local copies, waits for them, and re-layouts  62.1 us (7%)
  other arithmetic  27.5 us (3%)
  between operations  14.3 us (2%)
    unnamed x6, waiting for transfers between devices  216 us
    all_gather x1, waiting for transfers between devices, shards(): lax.all_gather(row_error, ('grp', 'tp', 'dp'), axis=0, tiled=True)  189 us
    psum x1, waiting for transfers between devices, shards(): attn_sum = lax.psum(partial_value, 'tp')  70.6 us
    dot_general x1, matrix products, shards(): jnp.einsum('tl,tmd->lmd', act_bf, errors, preferred_element_type=jnp.floa...  40.1 us
    all_gather x1, waiting for transfers between devices, shards(): stacked = lax.all_gather(layer_out[None], ('grp', 'dp'), axis=0, tiled=True)  38.8 us
    unnamed x19, local copies, waits for them, and re-layouts  34.5 us
    reduce_scatter x1, waiting for transfers between devices, shards(): lax.psum_scatter(jnp.dot(moved_normed, joined, preferred_element_type=jnp...  30.1 us
    dot_general x1, matrix products, shards(): jnp.einsum('tmd,lmd->tl', errors, coder_weight, preferred_element_type=jn...  28.2 us
  transfers between devices with their start and end apart: 5, of which 5 were waited for; matrix products, arithmetic and copies ran while one was open for 4% of the time, Pallas kernels for 0%

commit v1 on v0

--- a/solution.py
+++ b/solution.py
@@ -1,14 +1,362 @@
+import functools
 import jax
 import jax.numpy as jnp
 from jax import lax
+from jax.experimental import pallas as pl
+from jax.experimental.pallas import tpu as pltpu
 from jax.sharding import PartitionSpec as P
 
 HEAD_DIM = 128
 TOK_DEV = 64
-
+TOKENS = 512
+BLOCK = 512
+HALF = BLOCK // 2
+RING = 4
 
 sparsity = 1.0
 rope_base = 500000.0
+
+ROUTES = (
+    ((0, 32, "xyz"), (32, 16, "yzx"), (48, 16, "zxy")),
+    ((0, 32, "yzx"), (32, 16, "xyz"), (48, 16, "zxy")),
+)
+
+
+class Place:
+    def __init__(self):
+        self.m = lax.axis_index("grp")
+        tp, dp = lax.axis_index("tp"), lax.axis_index("dp")
+        self.tp, self.dp = tp, dp
+        self.core = lax.rem(dp, 2)
+        self.at = {"x": lax.div(dp, 2), "y": lax.div(tp, 2), "z": lax.rem(tp, 2) * 2 + self.m}
+
+    def device(self, at, core):
+        z = at["z"]
+        return (lax.rem(z, 2), at["y"] * 2 + lax.div(z, 2), at["x"] * 2 + core)
+
+    def beside(self, axis, step):
+        return lax.rem(self.at[axis] + (step + RING), RING)
+
+    def neighbour(self, axis, step):
+        return self.device({**self.at, axis: self.beside(axis, step)}, self.core)
+
+    def sibling(self):
+        return self.device(self.at, 1 - self.core)
+
+    def enter(self):
+        barrier = pltpu.get_barrier_semaphore()
+        for axis in "xyz":
+            for step in (1, -1):
+                pl.semaphore_signal(barrier, inc=1, device_id=self.neighbour(axis, step), device_id_type=pl.DeviceIdType.MESH)
+        pl.semaphore_signal(barrier, inc=1, device_id=self.sibling(), device_id_type=pl.DeviceIdType.MESH)
+        pl.semaphore_wait(barrier, 7)
+
+
+def part(buf, core, sel, rows, cols=(0, BLOCK)):
+    index = [] if core is None else [core]
+    z = sel.get("z")
+    if z is None:
+        index += [slice(None), slice(None)]
+    elif isinstance(z, int):
+        index += [z // 2, z % 2]
+    else:
+        index += [lax.div(z, 2), lax.rem(z, 2)]
+    for axis in "yx":
+        index.append(sel.get(axis, slice(None)))
+    index += [pl.ds(*rows), pl.ds(*cols)]
+    return buf.at[tuple(index)]
+
+
+LOW, HIGH = (0, HALF), (HALF, HALF)
+
+
+def send(src, dst, send_sem, recv_sem, device):
+    copy = pltpu.make_async_remote_copy(
+        src_ref=src, dst_ref=dst, send_sem=send_sem, recv_sem=recv_sem, device_id=device, device_id_type=pl.DeviceIdType.MESH
+    )
+    copy.start()
+    return copy
+
+
+def arrive(dst, sem, place):
+    pltpu.make_async_remote_copy(
+        src_ref=dst, dst_ref=dst, send_sem=sem, recv_sem=sem, device_id=place.sibling(), device_id_type=pl.DeviceIdType.MESH
+    ).wait_recv()
+
+
+def gather(place, core, buf, sems):
+    send_sems, recv_sems, give_sems, take_sems = sems
+    routes, other = ROUTES[core], ROUTES[1 - core]
+    sibling = place.sibling()
+    pending = []
+
+    def sel_of(order, k, v):
+        sel = {order[k]: v}
+        for axis in order[k + 1 :]:
+            sel[axis] = place.at[axis]
+        return sel
+
+    def give(i, j, sel, rows):
+        ref = part(buf, core, sel, rows)
+        pending.append(send(ref, ref, give_sems.at[i, j], take_sems.at[i, j], sibling))
+
+    for i, (r0, n, order) in enumerate(routes):
+        give(i, 9, dict(place.at), (r0, n))
+    for k in range(3):
+        for i, (r0, n, order) in enumerate(routes):
+            ref = part(buf, core, sel_of(order, k, place.at[order[k]]), (r0, n))
+            for j, step in enumerate((1, -1)):
+                pending.append(send(ref, ref, send_sems.at[i, k, j], recv_sems.at[i, k, j], place.neighbour(order[k], step)))
+        for i, (r0, n, order) in enumerate(routes):
+            axis = order[k]
+            for j, (step, cols) in enumerate(((1, LOW), (-1, HIGH))):
+                sel = sel_of(order, k, place.beside(axis, -step))
+                arrive(part(buf, core, sel, (r0, n)), recv_sems.at[i, k, j], place)
+                ref = part(buf, core, sel, (r0, n), cols)
+                pending.append(send(ref, ref, send_sems.at[i, k, 2 + j], recv_sems.at[i, k, 2 + j], place.neighbour(axis, step)))
+                give(i, k * 3 + j, sel, (r0, n))
+        for i, (r0, n, order) in enumerate(routes):
+            sel = sel_of(order, k, place.beside(order[k], 2))
+            for j, cols in enumerate((LOW, HIGH)):
+                arrive(part(buf, core, sel, (r0, n), cols), recv_sems.at[i, k, 2 + j], place)
+            give(i, k * 3 + 2, sel, (r0, n))
+    for i, (r0, n, order) in enumerate(other):
+        for k in range(3):
+            for j, v in enumerate((-1, 1, 2)):
+                arrive(part(buf, 1 - core, sel_of(order, k, place.beside(order[k], v)), (r0, n)), take_sems.at[i, k * 3 + j], place)
+        arrive(part(buf, 1 - core, dict(place.at), (r0, n)), take_sems.at[i, 9], place)
+    for copy in pending:
+        copy.wait_send()
+
+
+def spread(sel, i):
+    at, rest = {}, i
+    for axis in "xyz":
+        if sel.get(axis) is None:
+            at[axis] = lax.rem(rest, RING)
+            rest = lax.div(rest, RING)
+        else:
+            at[axis] = sel[axis]
+    z = at["z"]
+    zh, zl = (z // 2, z % 2) if isinstance(z, int) else (lax.div(z, 2), lax.rem(z, 2))
+    return zh, zl, at["y"], at["x"]
+
+
+def scatter_sum(place, core, sums, landing, result, sems):
+    send_sems, recv_sems = sems
+    routes = ROUTES[core]
+    pending = []
+
+    def sel_of(order, k, v, done):
+        sel = {order[k]: v}
+        for axis in order[:k]:
+            sel[axis] = done if done is not None else place.at[axis]
+        return sel
+
+    def add(order, k, target, slots, rows, cols, into_result):
+        sel = sel_of(order, k, target, None)
+        count = RING ** (2 - k)
+
+        def step(i, carry):
+            own = spread(sel, i)
+            window = (pl.ds(*rows), pl.ds(*cols))
+            total = sums[own + window].astype(jnp.float32)
+            for slot in slots:
+                total = total + landing[spread(sel_of(order, k, slot, 3), i) + window].astype(jnp.float32)
+            if into_result:
+                result[window] = total
+            else:
+                sums[own + window] = total.astype(jnp.bfloat16)
+            return carry
+
+        lax.fori_loop(0, count, step, 0)
+
+    for k in range(3):
+        for i, (r0, n, order) in enumerate(routes):
+            axis = order[k]
+            for j, (step, slot, v, cols) in enumerate(((1, 0, 2, LOW), (-1, 0, 2, HIGH), (1, 1, 1, HIGH), (-1, 2, -1, LOW))):
+                src = part(sums, None, sel_of(order, k, place.beside(axis, v), None), (r0, n), cols)
+                dst = part(landing, None, sel_of(order, k, slot, 3), (r0, n), cols)
+                pending.append(send(src, dst, send_sems.at[i, k, j], recv_sems.at[i, k, j], place.neighbour(axis, step)))
+        for i, (r0, n, order) in enumerate(routes):
+            axis = order[k]
+            for j, (step, slot, cols) in enumerate(((1, 1, LOW), (-1, 2, HIGH))):
+                arrive(part(landing, None, sel_of(order, k, 0, 3), (r0, n), cols), recv_sems.at[i, k, j], place)
+                add(order, k, place.beside(axis, step), (0,), (r0, n), cols, False)
+                src = part(sums, None, sel_of(order, k, place.beside(axis, step), None), (r0, n), cols)
+                dst = part(landing, None, sel_of(order, k, slot, 3), (r0, n), cols)
+                pending.append(send(src, dst, send_sems.at[i, k, 4 + j], recv_sems.at[i, k, 4 + j], place.neighbour(axis, step)))
+        for i, (r0, n, order) in enumerate(routes):
+            for j, (slot, cols) in ((2, (1, HIGH)), (3, (2, LOW)), (4, (1, LOW)), (5, (2, HIGH))):
+                arrive(part(landing, None, sel_of(order, k, slot, 3), (r0, n), cols), recv_sems.at[i, k, j], place)
+            add(order, k, place.at[order[k]], (1, 2), (r0, n), (0, BLOCK), k == 2)
+    for copy in pending:
+        copy.wait_send()
+
+
+def gelu_pair(pre_act):
+    normal_cdf = 0.5 * (1.0 + lax.erf(pre_act * 0.7071067811865476))
+    density = jnp.exp(-0.5 * pre_act * pre_act) * 0.3989422804014327
+    return (pre_act * normal_cdf, normal_cdf + pre_act * density)
+
+
+def nt(a, b):
+    return lax.dot_general(a, b, (((1,), (1,)), ((), ())), preferred_element_type=jnp.float32)
+
+
+def nn(a, b):
+    return lax.dot_general(a, b, (((1,), (0,)), ((), ())), preferred_element_type=jnp.float32)
+
+
+def chunk_of(k):
+    mm, x, c = lax.div(k, 8), lax.rem(lax.div(k, 2), RING), lax.rem(k, 2)
+    return mm, x, c, pl.ds(pl.multiple_of((x * 2 + c) * BLOCK, BLOCK), BLOCK)
+
+
+def token_rows(buf, mm, x, c):
+    return buf[c, :, mm, :, x].reshape(TOKENS, BLOCK)
+
+
+def coder_kernel(
+    own_ref, w_hbm, enc_ref, dec_ref,
+    gw_hbm, genc_ref, gdec_ref,
+    rows, errs, w, sums, give, taken, landing, result, total, act_t, act, slope, pre_t, norms, latsum, stage,
+    w_sem, rows_send, rows_recv, rows_give, rows_take, errs_send, errs_recv, errs_give, errs_take,
+    sum_send, sum_recv, pair_send, pair_recv, out_sem,
+):
+    place = Place()
+    m, core = place.m, place.core
+    load = pltpu.make_async_copy(w_hbm, w, w_sem)
+    load.start()
+    own = (lax.div(place.at["z"], 2), m, place.at["y"], place.at["x"])
+    rows[(core,) + own] = own_ref[...]
+    place.enter()
+    for c in (0, 1):
+        pl.when(core == c)(functools.partial(gather, place, c, rows, (rows_send, rows_recv, rows_give, rows_take)))
+    load.wait()
+
+    def norm_step(i, carry):
+        at = pl.ds(pl.multiple_of(i * 16, 16), 16)
+        for mm in (0, 1):
+            wide = w[mm, at, :].astype(jnp.float32)
+            norms[mm, at, :] = jnp.sqrt(jnp.sum(wide * wide, -1, keepdims=True) + 1e-06)
+        return carry
+
+    lax.fori_loop(0, TOKENS // 16, norm_step, 0)
+
+    def contract(buf):
+        total[...] = jnp.zeros_like(total)
+
+        def step(k, carry):
+            mm, x, c, cols = chunk_of(k)
+            total[...] += nt(w[mm, :, cols], token_rows(buf, mm, x, c))
+            return carry
+
+        lax.fori_loop(0, 16, step, 0)
+
+    contract(rows)
+    for l0 in range(0, BLOCK, 128):
+        at = pl.ds(l0, 128)
+        lat, slope[at, :] = gelu_pair(total[at, :] + enc_ref[at, :])
+        latsum[at, :] = jnp.sum(lat, -1, keepdims=True)
+        act_t[at, :] = lat.astype(jnp.bfloat16)
+        act[:, at] = lat.T.astype(jnp.bfloat16)
+
+    pairs = []
+    for k in range(8):
+        mm, x = k // 4, k % 4
+        cols = pl.ds(pl.multiple_of((x * 2 + 1 - core) * BLOCK, BLOCK), BLOCK)
+        give[:, mm, :, x] = nn(act[...], w[mm, :, cols]).astype(jnp.bfloat16).reshape(2, RING, TOK_DEV, BLOCK)
+        pairs.append(send(give.at[:, mm, :, x], taken.at[:, mm, :, x], pair_send.at[k], pair_recv.at[k], place.sibling()))
+    for k in range(8):
+        mm, x = k // 4, k % 4
+        cols = pl.ds(pl.multiple_of((x * 2 + core) * BLOCK, BLOCK), BLOCK)
+        here = nn(act[...], w[mm, :, cols])
+        pairs[k].wait_recv()
+        there = taken[:, mm, :, x].reshape(TOKENS, BLOCK).astype(jnp.float32)
+        sums[:, mm, :, x] = (here + there).astype(jnp.bfloat16).reshape(2, RING, TOK_DEV, BLOCK)
+    for copy in pairs:
+        copy.wait_send()
+    for c in (0, 1):
+        pl.when(core == c)(functools.partial(scatter_sum, place, c, sums, landing, result, (sum_send, sum_recv)))
+    bias = dec_ref[pl.ds(m * 8 + place.dp, 1), :]
+    errs[(core,) + own] = (result[...] + bias - own_ref[...].astype(jnp.float32)).astype(jnp.bfloat16)
+    for c in (0, 1):
+        pl.when(core == c)(functools.partial(gather, place, c, errs, (errs_send, errs_recv, errs_give, errs_take)))
+
+    contract(errs)
+    for l0 in range(0, BLOCK, 128):
+        at = pl.ds(l0, 128)
+        norm_total = norms[0, at, :] + norms[1, at, :]
+        pre_grad = (2.0 / TOKENS * total[at, :] + sparsity / TOKENS * norm_total) * slope[at, :]
+        genc_ref[at, :] = jnp.sum(pre_grad, -1, keepdims=True)
+        pre_t[at, :] = pre_grad.astype(jnp.bfloat16)
+
+    def grad_step(k, carry):
+        mm, x, c, cols = chunk_of(k)
+        slot = lax.rem(k, 2)
+        out = pltpu.make_async_copy(stage.at[slot], gw_hbm.at[mm, :, cols], out_sem.at[slot])
+        pl.when(k >= 2)(out.wait)
+        err = token_rows(errs, mm, x, c)
+        scale = sparsity / TOKENS * latsum[...] / norms[mm]
+        grad = 2.0 / TOKENS * nn(act_t[...], err) + nn(pre_t[...], token_rows(rows, mm, x, c))
+        stage[slot] = (grad + scale * w[mm, :, cols].astype(jnp.float32)).astype(jnp.bfloat16)
+        out.start()
+        ones = jnp.ones((16, TOKENS), jnp.bfloat16)
+        gdec_ref[pl.ds(mm, 1), cols] = 2.0 / TOKENS * nn(ones, err)[:1]
+        return carry
+
+    lax.fori_loop(0, 16, grad_step, 0)
+    for slot in (0, 1):
+        pltpu.make_async_copy(stage.at[slot], gw_hbm.at[1, :, pl.ds((6 + slot) * BLOCK, BLOCK)], out_sem.at[slot]).wait()
+
+
+def coder(own_rows, weight, enc_bias, dec_bias):
+    latents, features = weight.shape[1:]
+    blocks = (2, 2, RING, RING, TOK_DEV, BLOCK)
+    bf16, f32 = jnp.bfloat16, jnp.float32
+    dma = pltpu.SemaphoreType.DMA
+    vmem = pl.BlockSpec(memory_space=pltpu.VMEM)
+    hbm = pl.BlockSpec(memory_space=pl.ANY)
+    ring = [dma((3, 3, 4)), dma((3, 3, 4)), dma((3, 10)), dma((3, 10))]
+    return pl.pallas_call(
+        coder_kernel,
+        out_shape=(
+            jax.ShapeDtypeStruct((2, latents, features), bf16),
+            jax.ShapeDtypeStruct((latents, 1), f32),
+            jax.ShapeDtypeStruct((2, features), f32),
+        ),
+        in_specs=[vmem, hbm, vmem, vmem],
+        out_specs=(hbm, vmem, vmem),
+        scratch_shapes=[
+            pltpu.VMEM((2,) + blocks, bf16),
+            pltpu.VMEM((2,) + blocks, bf16),
+            pltpu.VMEM((2, latents, features), bf16),
+            pltpu.VMEM(blocks, bf16),
+            pltpu.VMEM(blocks, bf16),
+            pltpu.VMEM(blocks, bf16),
+            pltpu.VMEM(blocks, bf16),
+            pltpu.VMEM((TOK_DEV, BLOCK), f32),
+            pltpu.VMEM((latents, TOKENS), f32),
+            pltpu.VMEM((latents, TOKENS), bf16),
+            pltpu.VMEM((TOKENS, latents), bf16),
+            pltpu.VMEM((latents, TOKENS), f32),
+            pltpu.VMEM((latents, TOKENS), bf16),
+            pltpu.VMEM((2, latents, 1), f32),
+            pltpu.VMEM((latents, 1), f32),
+            pltpu.VMEM((2, latents, BLOCK), bf16),
+            dma(()),
+            *ring,
+            *ring,
+            dma((3, 3, 6)),
+            dma((3, 3, 6)),
+            dma((8,)),
+            dma((8,)),
+            dma((2,)),
+        ],
+        compiler_params=pltpu.CompilerParams(collective_id=0, has_side_effects=True, vmem_limit_bytes=60 * 1024 * 1024),
+        cost_estimate=pl.CostEstimate(flops=10 * TOKENS * latents * 2 * features, bytes_accessed=32 << 20, transcendentals=0),
+    )(own_rows, weight, enc_bias.reshape(latents, 1), dec_bias.reshape(16, BLOCK))
 
 
 def doc_layout(doc_lengths, token_index):
@@ -30,12 +378,6 @@
     return jnp.concatenate(
         [low_half * cosine - high_half * sine_vals, high_half * cosine + low_half * sine_vals], -1
     )
-
-
-def gelu_pair(pre_act):
-    normal_cdf = 0.5 * (1.0 + lax.erf(pre_act * 0.7071067811865476))
-    density = jnp.exp(-0.5 * pre_act * pre_act) * 0.3989422804014327
-    return (pre_act * normal_cdf, normal_cdf + pre_act * density)
 
 
 def shards(
@@ -113,72 +455,11 @@
     )
     every_mixed = lax.all_gather(head_mixed, "dp", axis=0, tiled=True)
     partial_value = jnp.dot(every_mixed, w_output[0], preferred_element_type=jnp.float32)
-    attn_sum = lax.psum(partial_value, "tp")
-    layer_out = (moved_rows.astype(jnp.float32) + attn_sum).astype(jnp.bfloat16)
-    col_width = layer_out.shape[1]
-    stacked = lax.all_gather(layer_out[None], ("grp", "dp"), axis=0, tiled=True)
-    model_rows = (
-        stacked.reshape(2, dp_count, tokens_all, col_width)
-        .transpose(0, 2, 1, 3)
-        .reshape(2, tokens_all, dp_count * col_width)
-    )
-    model_width = model_rows.shape[2]
-    lat_here = coder_weight.shape[0]
-    pre_act = (
-        jnp.einsum("mtd,lmd->tl", model_rows, coder_weight, preferred_element_type=jnp.float32)
-        + enc_bias[None, :]
-    )
-    latent_act, act_slope = gelu_pair(pre_act)
-    act_bf = latent_act.astype(jnp.bfloat16)
-    devices = lax.axis_size(("grp", "tp", "dp"))
-    own_rows = tokens_all // devices
-    coder_flat = coder_weight.reshape(lat_here, 2 * model_width)
-    recon_rows = lax.psum_scatter(
-        jnp.dot(act_bf, coder_flat, preferred_element_type=jnp.float32),
-        ("grp", "tp", "dp"),
-        scatter_dimension=0,
-        tiled=True,
-    )
-    row_first = lax.axis_index(("grp", "tp", "dp")) * own_rows
-    target = (
-        lax.dynamic_slice_in_dim(model_rows, row_first, own_rows, 1)
-        .transpose(1, 0, 2)
-        .reshape(own_rows, 2 * model_width)
-    )
-    bias_flat = dec_bias.reshape(1, 2 * model_width)
-    row_error = (recon_rows + bias_flat - target.astype(jnp.float32)).astype(jnp.bfloat16)
-    errors = lax.all_gather(row_error, ("grp", "tp", "dp"), axis=0, tiled=True).reshape(
-        tokens_all, 2, model_width
-    )
-    weight_wide = coder_weight.astype(jnp.float32)
-    dec_norms = jnp.sqrt(jnp.sum(weight_wide * weight_wide, -1) + 1e-06)
-    norm_total = jnp.sum(dec_norms, -1)
-    act_grad = (
-        2.0
-        / tokens_all
-        * jnp.einsum("tmd,lmd->tl", errors, coder_weight, preferred_element_type=jnp.float32)
-        + sparsity / tokens_all * norm_total[None, :]
-    )
-    pre_grad = act_grad * act_slope
-    pre_grad_bf = pre_grad.astype(jnp.bfloat16)
-    weight_grad = (
-        2.0
-        / tokens_all
-        * jnp.einsum("tl,tmd->lmd", act_bf, errors, preferred_element_type=jnp.float32)
-    )
-    weight_grad = weight_grad + jnp.einsum(
-        "tl,mtd->lmd", pre_grad_bf, model_rows, preferred_element_type=jnp.float32
-    )
-    weight_grad = (
-        weight_grad
-        + sparsity
-        / tokens_all
-        * jnp.sum(latent_act, 0)[:, None, None]
-        * weight_wide
-        / dec_norms[:, :, None]
-    )
-    grad_dec_bias = 2.0 / tokens_all * jnp.sum(errors.astype(jnp.float32), 0)
-    return (weight_grad.astype(jnp.bfloat16), jnp.sum(pre_grad, 0), grad_dec_bias)
+    attn_sum = lax.psum_scatter(partial_value, "tp", scatter_dimension=0, tiled=True)
+    target = lax.dynamic_slice_in_dim(moved_rows, lax.axis_index("tp") * TOK_DEV, TOK_DEV, 0)
+    own_rows = (target.astype(jnp.float32) + attn_sum).astype(jnp.bfloat16)
+    weight_grad, grad_enc, grad_dec = coder(own_rows, coder_weight.transpose(1, 0, 2), enc_bias, dec_bias)
+    return (weight_grad.transpose(1, 0, 2), grad_enc.reshape(-1), grad_dec)
 
 
 def solution(mesh):

time: 830 us -> 355 us (0.43)
  waiting for transfers between devices: 544 us -> 80.2 us
  Pallas kernels: 0 us -> 153 us
  matrix products: 107 us -> 3.84 us
  local copies, waits for them, and re-layouts: 62.1 us -> 37.1 us
  other arithmetic: 27.5 us -> 5.49 us
  blocking collectives: 69.3 us -> 56.9 us
    all_gather x2 -> x0, waiting for transfers between devices: 228 us -> none  [the longest x1 189 us: shards(): lax.all_gather(row_error, ('grp', 'tp', 'dp'), axis=0, tiled=True)]
    unnamed x6 -> x2, waiting for transfers between devices: 216 us -> 0.03 us
    pallas_call x0 -> x1, Pallas kernels: none -> 153 us  [coder(): pl.pallas_call(coder_kernel, out_shape=(jax.ShapeDtypeStruct((2, latents,...]
    dot_general x5 -> x0, matrix products: 102 us -> none  [the longest x1 40.1 us: shards(): jnp.einsum('tl,tmd->lmd', act_bf, errors, preferred_element_type=jnp.floa...]
    psum x1 -> x0, waiting for transfers between devices: 70.6 us -> none  [shards(): attn_sum = lax.psum(partial_value, 'tp')]
    reduce_scatter x0 -> x1, waiting for transfers between devices: none -> 50.6 us  [shards(): lax.psum_scatter(partial_value, 'tp', scatter_dimension=0, tiled=True)]
    reshape x2, local copies, waits for them, and re-layouts: 23.9 us -> 1.51 us  [the longest x1 0.86 us: coder(): enc_bias.reshape(latents, 1)]
    reduce_sum x2 -> x0, other arithmetic: 19.6 us -> none  [the longest x1 12.2 us: shards(): dec_norms = jnp.sqrt(jnp.sum(weight_wide * weight_wide, -1) + 1e-06)]
  transfers between devices with their start and end apart: 5 -> 3, of which waited for: 5 -> 2; matrix products, arithmetic and copies ran while one was open for 4% -> 5% of each run, Pallas kernels for 0% -> 0%
where the time goes in v1:
time: 355 us; the launch traced here: 354 us
  Pallas kernels  153 us (43%)
  waiting for transfers between devices  80.2 us (23%)
  blocking collectives  56.9 us (16%)
  local copies, waits for them, and re-layouts  37.1 us (10%)
  between operations  14.2 us (4%)
  other arithmetic  5.49 us (2%)
  matrix products  3.84 us (1%)
  starting transfers between devices  3.64 us (1%)
    pallas_call x1, Pallas kernels, coder(): pl.pallas_call(coder_kernel, out_shape=(jax.ShapeDtypeStruct((2, latents,...  153 us
    reduce_scatter x1, waiting for transfers between devices, shards(): lax.psum_scatter(partial_value, 'tp', scatter_dimension=0, tiled=True)  50.6 us
    unnamed x23, local copies, waits for them, and re-layouts  31.8 us
    reduce_scatter x1, waiting for transfers between devices, shards(): lax.psum_scatter(jnp.dot(moved_normed, joined, preferred_element_type=jnp...  29.6 us
    all_gather x1, blocking collectives, shards(): lax.all_gather(keys_rot, 'dp', axis=0, tiled=True)  16.1 us
    all_to_all x1, blocking collectives, shards(): lax.all_to_all(normed, 'dp', split_axis=1, concat_axis=0, tiled=True)  15 us
    all_gather x1, blocking collectives, shards(): every_mixed = lax.all_gather(head_mixed, 'dp', axis=0, tiled=True)  13.1 us
    all_gather x1, blocking collectives, shards(): lax.all_gather(values_bf, 'dp', axis=0, tiled=True)  12.7 us
  transfers between devices with their start and end apart: 3, of which 2 were waited for; matrix products, arithmetic and copies ran while one was open for 5% of the time, Pallas kernels for 0%

profile of v1, /device:TPU:1, one launch (start us, length us, event | category | flops | bytes accessed | tf_op | source)
XLA Modules:
  0.0 354.0 jit_solution(663814599429850041)
XLA Ops:
  7.2 0.0 copy-start
  7.2 0.0 reduce-scatter.3.cloned.1.call-start
  7.2 1.3 multiply_reduce_fusion
  8.5 0.8 convert_reduce_fusion
  9.3 1.2 copy.50
  10.5 0.0 copy-start.6
  10.6 0.0 copy-start.7
  10.6 0.0 copy-start.8
  10.6 0.2 multiply_convert_fusion
  10.8 0.2 copy.41
  10.9 15.0 %all_to_all.35 = bf16[64,8,512]{2,0,1:T(8,128)(2,1)S(1)} all-to-all(bf16[64,8,512]{2,0,1:T(8,128)(2,1)S(1)} %copy.41), channel_id=1, replica_groups=mesh['grp'=2,'tp'=8,'dp'=8] {'dp'}, dimensions={1} | all-to-all | bytes 1048576 | tf_op jit(solution)/shard_map/all_to_all | solution.py:413
  25.9 0.0 copy-done.6
  25.9 0.0 copy-done.7
  25.9 0.0 copy-done.8
  25.9 1.7 fusion.5
  27.6 0.0 copy-start.5
  27.6 0.0 reduce-scatter.3.cloned.1.call-update
  27.7 0.0 reduce-scatter.5.cloned.1.call-start
  27.7 0.6 copy-done.5
  28.3 0.2 reduce-window.8
  28.5 0.1 convert_reduce_fusion.1
  28.6 0.1 fusion.31
  28.7 0.1 fusion.16
  28.8 0.2 multiply_cosine_fusion
  29.0 29.6 %reduce-scatter.3.cloned.1.call-done = f32[64,768]{1,0:T(8,128)} async-done(((f32[512,768]{1,0:T(8,128)}), f32[64,768]{1,0:T(8,128)}) %reduce-scatter.3.cloned.1.call-update) | async-done | bytes 196624 | tf_op jit(solution)/shard_map/reduce_scatter | solution.py:416
  58.5 0.8 slice_bitcast_fusion
  59.3 0.2 fusion.29
  59.5 0.9 slice.33
  60.5 0.1 pad_maximum_fusion
  60.6 16.1 %all_gather.10 = bf16[512,128]{1,0:T(8,128)(2,1)S(1)} all-gather(bf16[64,128]{1,0:T(8,128)(2,1)S(1)} %pad_maximum_fusion), channel_id=1, replica_groups=mesh['grp'=2,'tp'=8,'dp'=8] {'dp'}, dimensions={0}, use_global_device_ids=true | all-gather | bytes 147456 | tf_op jit(solution)/shard_map/all_gather | solution.py:440
  76.6 0.8 slice.50
  77.4 12.7 %all_gather.9 = bf16[512,128]{1,0:T(8,128)(2,1)S(1)} all-gather(bf16[64,128]{1,0:T(8,128)(2,1)S(1)} %slice.50), channel_id=1, replica_groups=mesh['grp'=2,'tp'=8,'dp'=8] {'dp'}, dimensions={0}, use_global_device_ids=true | all-gather | bytes 147456 | tf_op jit(solution)/shard_map/all_gather | solution.py:441
  90.1 0.1 fusion.34
  90.3 0.4 fusion.35
  90.7 0.3 fusion.4
  91.0 0.1 copy.44
  91.1 13.1 %all_gather.11 = bf16[512,512]{1,0:T(8,128)(2,1)S(1)} all-gather(bf16[64,512]{1,0:T(8,128)(2,1)S(1)} %bitcast.68), channel_id=1, replica_groups=mesh['grp'=2,'tp'=8,'dp'=8] {'dp'}, dimensions={0}, use_global_device_ids=true | all-gather | bytes 589824 | tf_op jit(solution)/shard_map/all_gather | solution.py:456
  104.2 0.0 copy-done
  104.2 1.4 fusion.11
  105.6 0.0 copy-start.2
  105.6 0.0 copy-start.4
  105.6 0.0 reduce-scatter.5.cloned.1.call-update
  105.7 1.0 copy.40
  106.6 3.6 %all-to-all-start = ((bf16[64,8,512]{2,0,1:T(8,128)(2,1)}), bf16[64,8,512]{2,0,1:T(8,128)(2,1)S(1)}, u32[]{:S(2)}, u32[]{:S(2)}) async-start(bf16[64,8,512]{2,0,1:T(8,128)(2,1)} %copy.40), calls=%async_computation | async-start | bytes 1048576 | tf_op jit(solution)/shard_map/all_to_all | solution.py:412
  110.2 0.0 copy-done.2
  110.2 0.6 reshape.237.dec_ref
  110.8 0.0 copy-done.4
  110.8 0.9 copy.46.enc_ref
  111.7 12.9 %copy.58 = bf16[512,2,4096]{2,0,1:T(8,128)(2,1)} copy(bf16[512,2,4096]{2,1,0:T(2,128)(2,1)} %param.17) | data formatting | bytes 16777216 | tf_op args[7]
  124.6 0.0 all-to-all-done
  124.6 50.6 %reduce-scatter.5.cloned.1.call-done = f32[64,512]{1,0:T(8,128)} async-done(((f32[512,512]{1,0:T(8,128)}), f32[64,512]{1,0:T(8,128)}) %reduce-scatter.5.cloned.1.call-update) | async-done | bytes 131088 | tf_op jit(solution)/shard_map/reduce_scatter | solution.py:458
  175.2 1.5 add_convert_fusion.own_ref
  176.8 152.6 %shard_map.121 = (bf16[2,512,4096]{2,1,0:T(8,128)(2,1)}, f32[512,1]{1,0:T(8,128)}, f32[2,4096]{1,0:T(2,128)}) custom-call(bf16[64,512]{1,0:T(8,128)(2,1)} %add_convert_fusion.own_ref, bf16[2,512,4096]{2,1,0:T(8,128)(2,1)} %bitcast.62, f32[512,1]{1,0:T(8,128)} %copy.46.enc_ref, f32[16,512]{1,0:T(8,128)} %reshape.237.dec_ref), custom_call_target="tpu_custom_call" | custom-call | flops 21474836480 | bytes 33554432 | tf_op jit(solution)/shard_map/pallas_call | solution.py:322
  329.4 0.0 copy-start.1
  329.4 0.0 copy-start.3
  329.4 16.4 %copy.47 = bf16[512,2,4096]{2,1,0:T(2,128)(2,1)} copy(bf16[512,2,4096]{2,0,1:T(8,128)(2,1)} %bitcast.63) | data formatting | bytes 16777216
  345.8 0.0 copy-done.1
  345.8 0.7 reduce.3
  346.5 0.0 copy-done.3
  346.5 0.6 copy.61
  (8 shorter events, 0.1 us)
Async XLA Ops:
  7.2 97.0 %copy-start = (bf16[1,512,512]{2,1,0:T(8,128)(2,1)S(1)}, bf16[1,512,512]{2,1,0:T(8,128)(2,1)}, u32[]{:S(2)}) copy-start(bf16[1,512,512]{2,1,0:T(8,128)(2,1)} %param.15) | copy-start | bytes 1572868
  7.2 51.4 %reduce-scatter.3.cloned.1.call-start = ((), (), s32[]{:S(2)}) async-start(), calls=%async_computation.4 | async-start | bytes 1769472 | tf_op jit(solution)/shard_map/reduce_scatter | solution.py:416
  10.5 15.4 %copy-start.6 = (bf16[1,512,512]{2,1,0:T(8,128)(2,1)S(1)}, bf16[1,512,512]{2,1,0:T(8,128)(2,1)}, u32[]{:S(2)}) copy-start(bf16[1,512,512]{2,1,0:T(8,128)(2,1)} %param.12) | copy-start | bytes 1572868
  10.6 15.3 %copy-start.7 = (bf16[1,512,128]{2,1,0:T(8,128)(2,1)S(1)}, bf16[1,512,128]{2,1,0:T(8,128)(2,1)}, u32[]{:S(2)}) copy-start(bf16[1,512,128]{2,1,0:T(8,128)(2,1)} %param.14) | copy-start | bytes 393220
  10.6 15.3 %copy-start.8 = (bf16[1,512,128]{2,1,0:T(8,128)(2,1)S(1)}, bf16[1,512,128]{2,1,0:T(8,128)(2,1)}, u32[]{:S(2)}) copy-start(bf16[1,512,128]{2,1,0:T(8,128)(2,1)} %param.13) | copy-start | bytes 393220
  27.6 0.7 copy-start.5
  27.7 147.6 %reduce-scatter.5.cloned.1.call-start = ((), (), s32[]{:S(2)}) async-start(), calls=%async_computation.5 | async-start | bytes 1179648 | tf_op jit(solution)/shard_map/reduce_scatter | solution.py:458
  105.6 4.6 %copy-start.2 = (f32[2,4096]{1,0:T(2,128)S(1)}, f32[2,4096]{1,0:T(2,128)}, u32[]{:S(2)}) copy-start(f32[2,4096]{1,0:T(2,128)} %param.19) | copy-start | bytes 98308
  105.6 5.2 %copy-start.4 = (f32[512]{0:T(512)S(1)}, f32[512]{0:T(512)}, u32[]{:S(2)}) copy-start(f32[512]{0:T(512)} %param.18) | copy-start | bytes 6148
  106.6 18.0 %all-to-all-start = ((bf16[64,8,512]{2,0,1:T(8,128)(2,1)}), bf16[64,8,512]{2,0,1:T(8,128)(2,1)S(1)}, u32[]{:S(2)}, u32[]{:S(2)}) async-start(bf16[64,8,512]{2,0,1:T(8,128)(2,1)} %copy.40), calls=%async_computation | async-start | bytes 1048576 | tf_op jit(solution)/shard_map/all_to_all | solution.py:412
  329.4 16.4 %copy-start.1 = (f32[512,1]{1,0:T(8,128)S(1)}, f32[512,1]{1,0:T(8,128)}, u32[]{:S(2)}) copy-start(f32[512,1]{1,0:T(8,128)} %get-tuple-element.7) | copy-start | bytes 6148
  329.4 17.2 %copy-start.3 = (f32[2,4096]{1,0:T(2,128)S(1)}, f32[2,4096]{1,0:T(2,128)}, u32[]{:S(2)}) copy-start(f32[2,4096]{1,0:T(2,128)} %get-tuple-element.41) | copy-start | bytes 98308
Sparse Core Ops, SparseCore 0:
  27.8 30.7 reduce-scatter.2
  105.8 69.3 reduce-scatter.4

commit v2 on v1

--- a/solution.py
+++ b/solution.py
@@ -1,6 +1,7 @@
 import functools
 import jax
 import jax.numpy as jnp
+import numpy as np
 from jax import lax
 from jax.experimental import pallas as pl
 from jax.experimental.pallas import tpu as pltpu
@@ -43,13 +44,18 @@
     def sibling(self):
         return self.device(self.at, 1 - self.core)
 
+    def dp_peer(self, j):
+        return (self.m, self.tp, lax.rem(self.dp + j, 8))
+
+    def tp_peer(self, j):
+        return (self.m, lax.rem(self.tp + j, 8), self.dp)
+
     def enter(self):
         barrier = pltpu.get_barrier_semaphore()
-        for axis in "xyz":
-            for step in (1, -1):
-                pl.semaphore_signal(barrier, inc=1, device_id=self.neighbour(axis, step), device_id_type=pl.DeviceIdType.MESH)
-        pl.semaphore_signal(barrier, inc=1, device_id=self.sibling(), device_id_type=pl.DeviceIdType.MESH)
-        pl.semaphore_wait(barrier, 7)
+        peers = [self.dp_peer(j) for j in range(1, 8)] + [self.tp_peer(j) for j in range(1, 8)]
+        for peer in peers + [self.neighbour("z", 1), self.neighbour("z", -1)]:
+            pl.semaphore_signal(barrier, inc=1, device_id=peer, device_id_type=pl.DeviceIdType.MESH)
+        pl.semaphore_wait(barrier, 16)
 
 
 def part(buf, core, sel, rows, cols=(0, BLOCK)):
@@ -217,23 +223,193 @@
     return buf[c, :, mm, :, x].reshape(TOKENS, BLOCK)
 
 
-def coder_kernel(
-    own_ref, w_hbm, enc_ref, dec_ref,
-    gw_hbm, genc_ref, gdec_ref,
-    rows, errs, w, sums, give, taken, landing, result, total, act_t, act, slope, pre_t, norms, latsum, stage,
+def doc_layout(lengths, token_index):
+    doc, start, end = jnp.zeros_like(token_index), jnp.zeros_like(token_index), 0
+    for i in range(4):
+        end = end + lengths[i]
+        passed = (token_index >= end).astype(jnp.int32)
+        doc, start = doc + passed, start + passed * lengths[i]
+    return doc, token_index - start
+
+
+def attend_layer(place, refs, bufs, sems, work):
+    res, gain, w_query, w_key, w_value, w_output, lengths, freq = refs
+    nsend, moved, raw, pair_out, pair_in, own_sum, qkv_out, qkv_in, kv, mixed, part_f, part_out, part_in = bufs
+    moved_s, moved_r, raw_s, raw_r, pair_s, pair_r, qkv_s, qkv_r, kv_s, kv_r, mixed_s, mixed_r, part_s, part_r = sems
+    dp, tp, core, x = place.dp, place.tp, place.core, place.at["x"]
+    pending = []
+
+    for r in range(0, TOK_DEV, 16):
+        wide = res[r : r + 16, :].astype(jnp.float32)
+        scale = lax.rsqrt(jnp.mean(wide * wide, -1, keepdims=True) + 1e-05)
+        normed = (wide * scale * gain[...].astype(jnp.float32)).astype(jnp.bfloat16)
+        for d in range(8):
+            nsend[d, r : r + 16, :] = normed[:, d * BLOCK : (d + 1) * BLOCK]
+    place.enter()
+    for j in range(1, 8):
+        there = lax.rem(dp + j, 8)
+        pending.append(send(nsend.at[there], moved.at[core, x], moved_s.at[j], moved_r.at[j], place.dp_peer(j)))
+    moved[core, x] = nsend[dp]
+
+    def columns(d):
+        return pl.ds(pl.multiple_of(d * BLOCK, BLOCK), BLOCK)
+
+    @pl.when(dp == tp)
+    def _():
+        for j in range(1, 8):
+            send(res.at[:, columns(lax.rem(dp + j, 8))], raw, raw_s.at[j], raw_r, place.dp_peer(j))
+        raw[...] = res[:, columns(dp)]
+
+    here = dp * TOK_DEV + lax.broadcasted_iota(jnp.int32, (TOK_DEV, 1), 0)
+    keys_at = lax.broadcasted_iota(jnp.int32, (1, TOKENS), 1)
+    doc, pos = doc_layout(lengths, here)
+    key_doc, _ = doc_layout(lengths, keys_at)
+    angles = pos.astype(jnp.float32) * freq[...]
+    lane = lax.broadcasted_iota(jnp.int32, (1, HEAD_DIM), 1)
+    cosine = jnp.cos(angles)
+    sine = jnp.sin(angles) * jnp.where(lane < HEAD_DIM // 2, -1.0, 1.0)
+    allowed = (doc == key_doc) & (keys_at <= here)
+    work(2)
+
+    for j in range(1, 8):
+        src = lax.rem(dp + 8 - j, 8)
+        arrive(moved.at[lax.rem(src, 2), lax.div(src, 2)], moved_r.at[j], place)
+
+    def project(c, out):
+        rows_in = moved[c].reshape(RING * TOK_DEV, BLOCK)
+        for w_ref, at, width in ((w_query, 0, 512), (w_key, 512, 128), (w_value, 640, 128)):
+            out[:, :, at : at + width] = nn(rows_in, w_ref[...]).reshape(RING, TOK_DEV, width)
+
+    project(1 - core, pair_out)
+    pair = send(pair_out, pair_in, pair_s, pair_r, place.sibling())
+    project(core, own_sum)
+    pair.wait_recv()
+    own_sum[...] = own_sum[...] + pair_in[...]
+    qkv_out[...] = own_sum[...].astype(jnp.bfloat16)
+    for j in range(1, RING):
+        there = lax.rem(x + j, RING)
+        pending.append(send(qkv_out.at[there], qkv_in.at[j], qkv_s.at[j], qkv_r.at[j], place.dp_peer(2 * j)))
+    work(2)
+    summed = own_sum[x]
+    for j in range(1, RING):
+        arrive(qkv_in.at[j], qkv_r.at[j], place)
+        summed = summed + qkv_in[j].astype(jnp.float32)
+
+    def rotate(values):
+        return (values * cosine + pltpu.roll(values, HEAD_DIM // 2, 1) * sine).astype(jnp.bfloat16)
+
+    kv[dp, :, :HEAD_DIM] = rotate(summed[:, 512:640])
+    kv[dp, :, HEAD_DIM:] = summed[:, 640:].astype(jnp.bfloat16)
+    for j in range(1, 8):
+        pending.append(send(kv.at[dp], kv.at[dp], kv_s.at[j], kv_r.at[j], place.dp_peer(j)))
+    query = jnp.concatenate([rotate(summed[:, h * HEAD_DIM : (h + 1) * HEAD_DIM]) for h in range(4)], 0)
+    work(1)
+    for j in range(1, 8):
+        arrive(kv.at[lax.rem(dp + 8 - j, 8)], kv_r.at[j], place)
+
+    all_kv = kv[...].reshape(TOKENS, 2 * HEAD_DIM)
+    scores = nt(query, all_kv[:, :HEAD_DIM]) * HEAD_DIM ** (-0.5)
+    mask = jnp.concatenate([allowed] * 4, 0)
+    terms = jnp.where(mask, jnp.exp(jnp.where(mask, scores, 0.0)), 0.0)
+    weights = (terms / jnp.sum(terms, -1, keepdims=True)).astype(jnp.bfloat16)
+    heads = nn(weights, all_kv[:, HEAD_DIM:]).astype(jnp.bfloat16)
+    for h in range(4):
+        mixed[dp, :, h * HEAD_DIM : (h + 1) * HEAD_DIM] = heads[h * TOK_DEV : (h + 1) * TOK_DEV]
+    for j in range(1, 8):
+        pending.append(send(mixed.at[dp], mixed.at[dp], mixed_s.at[j], mixed_r.at[j], place.dp_peer(j)))
+    work(2)
+    for j in range(1, 8):
+        arrive(mixed.at[lax.rem(dp + 8 - j, 8)], mixed_r.at[j], place)
+
+    outs = nn(mixed[...].reshape(TOKENS, BLOCK), w_output[...]).reshape(8, TOK_DEV, BLOCK)
+    part_f[...] = outs
+    part_out[...] = outs.astype(jnp.bfloat16)
+    for j in range(1, 8):
+        there = lax.rem(tp + j, 8)
+        pending.append(send(part_out.at[there], part_in.at[j], part_s.at[j], part_r.at[j], place.tp_peer(j)))
+    work(1)
+
+    @pl.when(dp != tp)
+    def _():
+        arrive(raw, raw_r, place)
+
+    total = part_f[tp]
+    for j in range(1, 8):
+        arrive(part_in.at[j], part_r.at[j], place)
+        total = total + part_in[j].astype(jnp.float32)
+
+    @pl.when(dp == tp)
+    def _():
+        for j in range(1, 8):
+            pltpu.make_async_remote_copy(
+                src_ref=res.at[:, columns(lax.rem(dp + j, 8))], dst_ref=raw, send_sem=raw_s.at[j], recv_sem=raw_r,
+                device_id=place.dp_peer(j), device_id_type=pl.DeviceIdType.MESH,
+            ).wait_send()
+
+    pair.wait_send()
+    for copy in pending:
+        copy.wait_send()
+    return (raw[...].astype(jnp.float32) + total).astype(jnp.bfloat16)
+
+
+def column_of(row):
+    return jnp.broadcast_to(row, (128, 128)).T[:, :1]
+
+
+def row_of(column):
+    return jnp.broadcast_to(column, (128, 128)).T[:1]
+
+
+SPLIT = 64
+
+
+def step_kernel(
+    res, gain, w_query, w_key, w_value, w_output, lengths, freq, w_hbm, enc_ref, dec_ref,
+    rows_hbm, errs_hbm, w_out, act_t, pre_t, scale_ref, genc_ref,
+    nsend, moved, raw, pair_out, pair_in, own_sum, qkv_out, qkv_in, kv, mixed, part_f, part_out, part_in,
+    own_ref, rows, errs, w_raw, w, sums, give, taken, landing, result, total, act, slope, norms, latsum,
+    moved_s, moved_r, raw_s, raw_r, pair_s, pair_r, qkv_s, qkv_r, kv_s, kv_r, mixed_s, mixed_r, part_s, part_r,
     w_sem, rows_send, rows_recv, rows_give, rows_take, errs_send, errs_recv, errs_give, errs_take,
     sum_send, sum_recv, pair_send, pair_recv, out_sem,
 ):
     place = Place()
     m, core = place.m, place.core
-    load = pltpu.make_async_copy(w_hbm, w, w_sem)
-    load.start()
+    loads = [
+        pltpu.make_async_copy(w_hbm.at[pl.ds(i * SPLIT, SPLIT)], w_raw.at[i % 2], w_sem.at[i % 2])
+        for i in range(BLOCK // SPLIT)
+    ]
+    loads[0].start()
+    loads[1].start()
+    done = [0]
+
+    def work(count):
+        for i in range(done[0], done[0] + count):
+            at = pl.ds(i * SPLIT, SPLIT)
+            loads[i].wait()
+
+            def step(k, carry):
+                cols = pl.ds(pl.multiple_of(k * BLOCK, BLOCK), BLOCK)
+                for mm in (0, 1):
+                    w[mm, at, cols] = w_raw[i % 2, :, mm, cols]
+                return carry
+
+            lax.fori_loop(0, 8, step, 0)
+            if i + 2 < len(loads):
+                loads[i + 2].start()
+        done[0] += count
+
+    layer_bufs = (nsend, moved, raw, pair_out, pair_in, own_sum, qkv_out, qkv_in, kv, mixed, part_f, part_out, part_in)
+    layer_sems = (moved_s, moved_r, raw_s, raw_r, pair_s, pair_r, qkv_s, qkv_r, kv_s, kv_r, mixed_s, mixed_r, part_s, part_r)
+    layer_refs = (res, gain, w_query, w_key, w_value, w_output, lengths, freq)
+    own_ref[...] = attend_layer(place, layer_refs, layer_bufs, layer_sems, work)
+    outs = [pltpu.make_async_copy(w, w_out, out_sem.at[0])]
+    outs[0].start()
     own = (lax.div(place.at["z"], 2), m, place.at["y"], place.at["x"])
     rows[(core,) + own] = own_ref[...]
-    place.enter()
     for c in (0, 1):
         pl.when(core == c)(functools.partial(gather, place, c, rows, (rows_send, rows_recv, rows_give, rows_take)))
-    load.wait()
+    outs.append(pltpu.make_async_copy(rows, rows_hbm, out_sem.at[1]))
+    outs[1].start()
 
     def norm_step(i, carry):
         at = pl.ds(pl.multiple_of(i * 16, 16), 16)
@@ -255,9 +431,9 @@
         lax.fori_loop(0, 16, step, 0)
 
     contract(rows)
-    for l0 in range(0, BLOCK, 128):
-        at = pl.ds(l0, 128)
-        lat, slope[at, :] = gelu_pair(total[at, :] + enc_ref[at, :])
+    for i in range(4):
+        at = pl.ds(i * 128, 128)
+        lat, slope[at, :] = gelu_pair(total[at, :] + column_of(enc_ref[i : i + 1, :]))
         latsum[at, :] = jnp.sum(lat, -1, keepdims=True)
         act_t[at, :] = lat.astype(jnp.bfloat16)
         act[:, at] = lat.T.astype(jnp.bfloat16)
@@ -283,183 +459,130 @@
     errs[(core,) + own] = (result[...] + bias - own_ref[...].astype(jnp.float32)).astype(jnp.bfloat16)
     for c in (0, 1):
         pl.when(core == c)(functools.partial(gather, place, c, errs, (errs_send, errs_recv, errs_give, errs_take)))
+    outs.append(pltpu.make_async_copy(errs, errs_hbm, out_sem.at[2]))
+    outs[2].start()
 
     contract(errs)
-    for l0 in range(0, BLOCK, 128):
-        at = pl.ds(l0, 128)
+    for i in range(4):
+        at = pl.ds(i * 128, 128)
         norm_total = norms[0, at, :] + norms[1, at, :]
         pre_grad = (2.0 / TOKENS * total[at, :] + sparsity / TOKENS * norm_total) * slope[at, :]
-        genc_ref[at, :] = jnp.sum(pre_grad, -1, keepdims=True)
+        genc_ref[i : i + 1, :] = row_of(jnp.sum(pre_grad, -1, keepdims=True))
         pre_t[at, :] = pre_grad.astype(jnp.bfloat16)
-
-    def grad_step(k, carry):
-        mm, x, c, cols = chunk_of(k)
-        slot = lax.rem(k, 2)
-        out = pltpu.make_async_copy(stage.at[slot], gw_hbm.at[mm, :, cols], out_sem.at[slot])
-        pl.when(k >= 2)(out.wait)
-        err = token_rows(errs, mm, x, c)
-        scale = sparsity / TOKENS * latsum[...] / norms[mm]
-        grad = 2.0 / TOKENS * nn(act_t[...], err) + nn(pre_t[...], token_rows(rows, mm, x, c))
-        stage[slot] = (grad + scale * w[mm, :, cols].astype(jnp.float32)).astype(jnp.bfloat16)
-        out.start()
+    scale_ref[...] = sparsity / TOKENS * latsum[...] / norms[...]
+    for copy in outs:
+        copy.wait()
+
+
+def grad_kernel(rows, errs, w, act_t, pre_t, scale, genc, gw, genc_out, gdec):
+    for mm in (0, 1):
+        err = errs[0, :, mm, :, 0].reshape(TOKENS, BLOCK)
+        grad = 2.0 / TOKENS * nn(act_t[...], err) + nn(pre_t[...], rows[0, :, mm, :, 0].reshape(TOKENS, BLOCK))
+        gw[:, mm, :] = (grad + scale[mm] * w[mm].astype(jnp.float32)).astype(jnp.bfloat16)
         ones = jnp.ones((16, TOKENS), jnp.bfloat16)
-        gdec_ref[pl.ds(mm, 1), cols] = 2.0 / TOKENS * nn(ones, err)[:1]
-        return carry
-
-    lax.fori_loop(0, 16, grad_step, 0)
-    for slot in (0, 1):
-        pltpu.make_async_copy(stage.at[slot], gw_hbm.at[1, :, pl.ds((6 + slot) * BLOCK, BLOCK)], out_sem.at[slot]).wait()
-
-
-def coder(own_rows, weight, enc_bias, dec_bias):
-    latents, features = weight.shape[1:]
+        gdec[mm : mm + 1, :] = 2.0 / TOKENS * nn(ones, err)[:1]
+    genc_out[...] = genc[...]
+
+
+def shards(
+    residual, norm_gain, w_query, w_key, w_value, w_output, doc_lengths, coder_weight, enc_bias, dec_bias
+):
+    latents, _, features = coder_weight.shape
     blocks = (2, 2, RING, RING, TOK_DEV, BLOCK)
     bf16, f32 = jnp.bfloat16, jnp.float32
-    dma = pltpu.SemaphoreType.DMA
+    dma, vm = pltpu.SemaphoreType.DMA, pltpu.VMEM
     vmem = pl.BlockSpec(memory_space=pltpu.VMEM)
     hbm = pl.BlockSpec(memory_space=pl.ANY)
     ring = [dma((3, 3, 4)), dma((3, 3, 4)), dma((3, 10)), dma((3, 10))]
-    return pl.pallas_call(
-        coder_kernel,
+    half = np.arange(HEAD_DIM // 2)
+    freq = np.concatenate([rope_base ** (-half * 2.0 / HEAD_DIM)] * 2)[None].astype(np.float32)
+    block = (TOK_DEV, BLOCK)
+    rows, errs, w_t, act_t, pre_t, scale, genc = pl.pallas_call(
+        step_kernel,
         out_shape=(
+            jax.ShapeDtypeStruct((2,) + blocks, bf16),
+            jax.ShapeDtypeStruct((2,) + blocks, bf16),
             jax.ShapeDtypeStruct((2, latents, features), bf16),
-            jax.ShapeDtypeStruct((latents, 1), f32),
-            jax.ShapeDtypeStruct((2, features), f32),
+            jax.ShapeDtypeStruct((latents, TOKENS), bf16),
+            jax.ShapeDtypeStruct((latents, TOKENS), bf16),
+            jax.ShapeDtypeStruct((2, latents, 1), f32),
+            jax.ShapeDtypeStruct((4, 128), f32),
         ),
-        in_specs=[vmem, hbm, vmem, vmem],
-        out_specs=(hbm, vmem, vmem),
+        in_specs=[vmem] * 6 + [pl.BlockSpec(memory_space=pltpu.SMEM), vmem, hbm, vmem, vmem],
+        out_specs=(hbm, hbm, hbm, vmem, vmem, vmem, vmem),
         scratch_shapes=[
-            pltpu.VMEM((2,) + blocks, bf16),
-            pltpu.VMEM((2,) + blocks, bf16),
-            pltpu.VMEM((2, latents, features), bf16),
-            pltpu.VMEM(blocks, bf16),
-            pltpu.VMEM(blocks, bf16),
-            pltpu.VMEM(blocks, bf16),
-            pltpu.VMEM(blocks, bf16),
-            pltpu.VMEM((TOK_DEV, BLOCK), f32),
-            pltpu.VMEM((latents, TOKENS), f32),
-            pltpu.VMEM((latents, TOKENS), bf16),
-            pltpu.VMEM((TOKENS, latents), bf16),
-            pltpu.VMEM((latents, TOKENS), f32),
-            pltpu.VMEM((latents, TOKENS), bf16),
-            pltpu.VMEM((2, latents, 1), f32),
-            pltpu.VMEM((latents, 1), f32),
-            pltpu.VMEM((2, latents, BLOCK), bf16),
-            dma(()),
+            vm((8,) + block, bf16),
+            vm((2, RING) + block, bf16),
+            vm(block, bf16),
+            vm((RING, TOK_DEV, 768), f32),
+            vm((RING, TOK_DEV, 768), f32),
+            vm((RING, TOK_DEV, 768), f32),
+            vm((RING, TOK_DEV, 768), bf16),
+            vm((RING, TOK_DEV, 768), bf16),
+            vm((8, TOK_DEV, 2 * HEAD_DIM), bf16),
+            vm((8,) + block, bf16),
+            vm((8,) + block, f32),
+            vm((8,) + block, bf16),
+            vm((8,) + block, bf16),
+            vm(block, bf16),
+            vm((2,) + blocks, bf16),
+            vm((2,) + blocks, bf16),
+            vm((2, SPLIT, 2, features), bf16),
+            vm((2, latents, features), bf16),
+            vm(blocks, bf16),
+            vm(blocks, bf16),
+            vm(blocks, bf16),
+            vm(blocks, bf16),
+            vm(block, f32),
+            vm((latents, TOKENS), f32),
+            vm((TOKENS, latents), bf16),
+            vm((latents, TOKENS), f32),
+            vm((2, latents, 1), f32),
+            vm((latents, 1), f32),
+            *[dma((8,)), dma((8,)), dma((8,)), dma(()), dma(()), dma(())],
+            *[dma((8,)) for _ in range(8)],
+            dma((2,)),
             *ring,
             *ring,
             dma((3, 3, 6)),
             dma((3, 3, 6)),
             dma((8,)),
             dma((8,)),
-            dma((2,)),
+            dma((3,)),
         ],
-        compiler_params=pltpu.CompilerParams(collective_id=0, has_side_effects=True, vmem_limit_bytes=60 * 1024 * 1024),
-        cost_estimate=pl.CostEstimate(flops=10 * TOKENS * latents * 2 * features, bytes_accessed=32 << 20, transcendentals=0),
-    )(own_rows, weight, enc_bias.reshape(latents, 1), dec_bias.reshape(16, BLOCK))
-
-
-def doc_layout(doc_lengths, token_index):
-    doc_ends = jnp.cumsum(doc_lengths)
-    passed = (token_index[:, None] >= doc_ends[None, :]).astype(jnp.int32)
-    doc_ids = jnp.sum(passed, axis=1)
-    doc_start = jnp.sum(passed * doc_lengths[None, :], axis=1)
-    return (doc_ids, token_index - doc_start)
-
-
-def rotate(values, position):
-    half_dim = values.shape[-1] // 2
-    inv_freq = rope_base ** (-jnp.arange(half_dim, dtype=jnp.float32) * 2.0 / values.shape[-1])
-    angles = position.astype(jnp.float32)[:, None] * inv_freq[None, :]
-    cosine = jnp.cos(angles)[:, None, :]
-    sine_vals = jnp.sin(angles)[:, None, :]
-    low_half = values[..., :half_dim]
-    high_half = values[..., half_dim:]
-    return jnp.concatenate(
-        [low_half * cosine - high_half * sine_vals, high_half * cosine + low_half * sine_vals], -1
+        compiler_params=pltpu.CompilerParams(collective_id=0, has_side_effects=True, vmem_limit_bytes=62 * 1024 * 1024),
+        cost_estimate=pl.CostEstimate(flops=6 * TOKENS * latents * 2 * features, bytes_accessed=40 << 20, transcendentals=0),
+    )(
+        residual[0], norm_gain, w_query[0], w_key[0], w_value[0], w_output[0], doc_lengths, jnp.asarray(freq),
+        coder_weight, enc_bias.reshape(4, 128), dec_bias.reshape(16, BLOCK),
     )
-
-
-def shards(
-    residual,
-    norm_gain,
-    w_query,
-    w_key,
-    w_value,
-    w_output,
-    doc_lengths,
-    coder_weight,
-    enc_bias,
-    dec_bias,
-):
-    dp_count = lax.axis_size("dp")
-    tokens_all = dp_count * TOK_DEV
-    dp_here = lax.axis_index("dp")
-    own_index = dp_here * TOK_DEV + jnp.arange(TOK_DEV, dtype=jnp.int32)
-    key_index = jnp.arange(tokens_all, dtype=jnp.int32)
-    own_doc, own_pos = doc_layout(doc_lengths, own_index)
-    key_doc, key_pos = doc_layout(doc_lengths, key_index)
-    inputs = residual[0]
-    inputs_wide = inputs.astype(jnp.float32)
-    normed = (
-        inputs_wide
-        * lax.rsqrt(jnp.mean(inputs_wide * inputs_wide, -1, keepdims=True) + 1e-05)
-        * norm_gain[0].astype(jnp.float32)
-    ).astype(jnp.bfloat16)
-    query_cols = w_query.shape[2]
-    key_cols = w_key.shape[2]
-    moved_rows, moved_normed = (
-        lax.all_to_all(inputs, "dp", split_axis=1, concat_axis=0, tiled=True),
-        lax.all_to_all(normed, "dp", split_axis=1, concat_axis=0, tiled=True),
-    )
-    joined = jnp.concatenate([w_query[0], w_key[0], w_value[0]], 1)
-    summed = lax.psum_scatter(
-        jnp.dot(moved_normed, joined, preferred_element_type=jnp.float32),
-        "dp",
-        scatter_dimension=0,
-        tiled=True,
-    )
-    query_sum = summed[:, :query_cols]
-    keys_sum = summed[:, query_cols : query_cols + key_cols]
-    values_sum = summed[:, query_cols + key_cols :]
-    heads_here = query_cols // HEAD_DIM
-    kv_here = key_cols // HEAD_DIM
-    group_size = heads_here // kv_here
-    query_rot = (
-        rotate(query_sum.reshape(TOK_DEV, heads_here, HEAD_DIM), own_pos)
-        .astype(jnp.bfloat16)
-        .reshape(TOK_DEV, kv_here, group_size, HEAD_DIM)
-    )
-    keys_rot = (
-        rotate(keys_sum.reshape(TOK_DEV, kv_here, HEAD_DIM), own_pos)
-        .astype(jnp.bfloat16)
-        .reshape(TOK_DEV, key_cols)
-    )
-    values_bf = values_sum.astype(jnp.bfloat16)
-    all_keys, all_values = (
-        lax.all_gather(keys_rot, "dp", axis=0, tiled=True),
-        lax.all_gather(values_bf, "dp", axis=0, tiled=True),
-    )
-    all_keys = all_keys.reshape(tokens_all, kv_here, HEAD_DIM)
-    all_values = all_values.reshape(tokens_all, kv_here, HEAD_DIM)
-    scores = jnp.einsum(
-        "qkgh,skh->kgqs", query_rot, all_keys, preferred_element_type=jnp.float32
-    ) * HEAD_DIM ** (-0.5)
-    allowed = (own_doc[:, None] == key_doc[None, :]) & (key_index[None, :] <= own_index[:, None])
-    exp_terms = jnp.where(allowed, jnp.exp(jnp.where(allowed, scores, 0.0)), 0.0)
-    weights = (exp_terms / jnp.sum(exp_terms, -1, keepdims=True)).astype(jnp.bfloat16)
-    head_mixed = (
-        jnp.einsum("kgqs,skh->qkgh", weights, all_values, preferred_element_type=jnp.float32)
-        .astype(jnp.bfloat16)
-        .reshape(TOK_DEV, query_cols)
-    )
-    every_mixed = lax.all_gather(head_mixed, "dp", axis=0, tiled=True)
-    partial_value = jnp.dot(every_mixed, w_output[0], preferred_element_type=jnp.float32)
-    attn_sum = lax.psum_scatter(partial_value, "tp", scatter_dimension=0, tiled=True)
-    target = lax.dynamic_slice_in_dim(moved_rows, lax.axis_index("tp") * TOK_DEV, TOK_DEV, 0)
-    own_rows = (target.astype(jnp.float32) + attn_sum).astype(jnp.bfloat16)
-    weight_grad, grad_enc, grad_dec = coder(own_rows, coder_weight.transpose(1, 0, 2), enc_bias, dec_bias)
-    return (weight_grad.transpose(1, 0, 2), grad_enc.reshape(-1), grad_dec)
+    set_spec = pl.BlockSpec((1, 2, 2, RING, 1) + block, lambda k: (lax.rem(k, 2), 0, 0, 0, lax.div(k, 2), 0, 0))
+    whole = lambda *shape: pl.BlockSpec(shape, lambda k: (0,) * len(shape))
+    weight_grad, grad_enc, grad_dec = pl.pallas_call(
+        grad_kernel,
+        grid=(8,),
+        out_shape=(
+            jax.ShapeDtypeStruct((latents, 2, features), bf16),
+            jax.ShapeDtypeStruct((4, 128), f32),
+            jax.ShapeDtypeStruct((2, features), f32),
+        ),
+        in_specs=[
+            set_spec,
+            set_spec,
+            pl.BlockSpec((2, latents, BLOCK), lambda k: (0, 0, k)),
+            whole(latents, TOKENS),
+            whole(latents, TOKENS),
+            whole(2, latents, 1),
+            whole(4, 128),
+        ],
+        out_specs=(
+            pl.BlockSpec((latents, 2, BLOCK), lambda k: (0, 0, k)),
+            whole(4, 128),
+            pl.BlockSpec((2, BLOCK), lambda k: (0, k)),
+        ),
+        compiler_params=pltpu.CompilerParams(vmem_limit_bytes=48 * 1024 * 1024),
+    )(rows, errs, w_t, act_t, pre_t, scale, genc)
+    return (weight_grad, grad_enc.reshape(-1), grad_dec)
 
 
 def solution(mesh):

time: 355 us -> 209 us (0.59)
  waiting for transfers between devices: 80.2 us -> 0 us
  blocking collectives: 56.9 us -> 0 us
  Pallas kernels: 153 us -> 203 us
  local copies, waits for them, and re-layouts: 37.1 us -> 5.14 us
  between operations: 14.2 us -> 0.65 us
  other arithmetic: 5.49 us -> 0 us
  matrix products: 3.84 us -> 0 us
  starting transfers between devices: 3.64 us -> 0 us
    reduce_scatter x2 -> x0, waiting for transfers between devices: 80.2 us -> none  [the longest x1 50.6 us: shards(): lax.psum_scatter(partial_value, 'tp', scatter_dimension=0, tiled=True)]
    pallas_call x1 -> x2, Pallas kernels: 153 us -> 203 us  [the longest x1 184 us: shards(): pl.pallas_call(step_kernel, out_shape=(jax.ShapeDtypeStruct((2,) + blocks...]
    all_gather x3 -> x0, blocking collectives: 41.9 us -> none  [the longest x1 16.1 us: shards(): lax.all_gather(keys_rot, 'dp', axis=0, tiled=True)]
    unnamed x23 -> x8, local copies, waits for them, and re-layouts: 31.8 us -> 3.74 us
    all_to_all x1 -> x0, blocking collectives: 15 us -> none  [shards(): lax.all_to_all(normed, 'dp', split_axis=1, concat_axis=0, tiled=True)]
    dot_general x4 -> x0, matrix products: 3.84 us -> none  [the longest x1 1.72 us: shards(): jnp.dot(moved_normed, joined, preferred_element_type=jnp.float32)]
    all_to_all x1 -> x0, starting transfers between devices: 3.56 us -> none  [shards(): lax.all_to_all(inputs, 'dp', split_axis=1, concat_axis=0, tiled=True)]
  transfers between devices with their start and end apart: 3 -> 0, of which waited for: 2 -> 0; matrix products, arithmetic and copies ran while one was open for 5% -> 0% of each run, Pallas kernels for 0% -> 0%
where the time goes in v2:
time: 209 us
  Pallas kernels  203 us (97%)
  local copies, waits for them, and re-layouts  5.14 us (2%)
    pallas_call x1, Pallas kernels, shards(): pl.pallas_call(step_kernel, out_shape=(jax.ShapeDtypeStruct((2,) + blocks...  184 us
    pallas_call x1, Pallas kernels, shards(): pl.pallas_call(grad_kernel, grid=(8,), out_shape=(jax.ShapeDtypeStruct((l...  19.2 us

profile of v2, /device:TPU:1, one launch (start us, length us, event | category | flops | bytes accessed | tf_op | source)
XLA Modules:
  0.0 208.6 jit_solution(16129579238809295295)
XLA Ops:
  0.6 1.4 reshape.16.dec_ref
  2.0 183.7 %shard_map.130 = (bf16[2,2,2,4,4,64,512]{6,5,4,3,2,1,0:T(8,128)(2,1)}, bf16[2,2,2,4,4,64,512]{6,5,4,3,2,1,0:T(8,128)(2,1)}, bf16[2,512,4096]{2,1,0:T(8,128)(2,1)...) custom-call(bf16[64,4096]{1,0:T(8,128)(2,1)} %bitcast.7, ...), custom_call_target="tpu_custom_call" | custom-call | flops 12884901888 | bytes 41943040 | tf_op jit(solution)/shard_map/pallas_call | solution.py:500
  185.7 0.0 copy-start
  185.7 1.0 copy-done
  186.8 0.0 copy-start.1
  186.8 1.0 copy-done.1
  187.8 0.0 copy-start.2
  187.8 1.0 copy-done.2
  188.9 0.0 copy-start.3
  188.9 0.6 copy-done.3
  189.5 19.2 %shard_map.131 = (bf16[512,2,4096]{2,1,0:T(2,128)(2,1)}, f32[4,128]{1,0:T(4,128)}, f32[2,4096]{1,0:T(2,128)}) custom-call(bf16[2,2,2,4,4,64,512]{6,5,4,3,2,1,0:T(8,128)(2,1)} %get-tuple-element.13.rows, bf16[2,2,2,4,4,64,512]{6,5,4,3,2,1,0:T(8,128)(2,1)} %get-tuple-element.14.errs, bf16[2,512,4096]{2,1,0:T(8,128)(2,1)} %get-tuple-element.15.w, ...), custom_call_target="tpu_custom_call" | custom-call | tf_op jit(solution)/shard_map/pallas_call | solution.py:561
Async XLA Ops:
  185.7 1.0 copy-start
  186.8 1.0 copy-start.1
  187.8 1.0 copy-start.2
  188.9 0.6 copy-start.3

commit v3 on v2

v3 whole, which is shorter than its diff:
```python
import functools
import jax
import jax.numpy as jnp
import numpy as np
from jax import lax
from jax.experimental import pallas as pl
from jax.experimental.pallas import tpu as pltpu
from jax.sharding import PartitionSpec as P

HEAD_DIM = 128
TOK_DEV = 64
TOKENS = 512
BLOCK = 512
RING = 4
HALF = TOK_DEV // 2
HALF_TOKENS = TOKENS // 2

sparsity = 1.0
rope_base = 500000.0

ROUTES = (((0, 16), (0, 384), "xyz"), ((16, 16), (0, 384), "yzx"), ((0, 32), (384, 128), "zxy"))


class Place:
    def __init__(self):
        self.m = lax.axis_index("grp")
        tp, dp = lax.axis_index("tp"), lax.axis_index("dp")
        self.tp, self.dp = tp, dp
        self.core = lax.rem(dp, 2)
        self.at = {"x": lax.div(dp, 2), "y": lax.div(tp, 2), "z": lax.rem(tp, 2) * 2 + self.m}

    def device(self, at, core):
        z = at["z"]
        return (lax.rem(z, 2), at["y"] * 2 + lax.div(z, 2), at["x"] * 2 + core)

    def beside(self, axis, step):
        return lax.rem(self.at[axis] + (step + RING), RING)

    def neighbour(self, axis, step):
        return self.device({**self.at, axis: self.beside(axis, step)}, self.core)

    def sibling(self):
        return self.device(self.at, 1 - self.core)

    def dp_peer(self, j):
        return (self.m, self.tp, lax.rem(self.dp + j, 8))

    def tp_peer(self, j):
        return (self.m, lax.rem(self.tp + j, 8), self.dp)

    def enter(self):
        barrier = pltpu.get_barrier_semaphore()
        peers = [self.dp_peer(j) for j in range(1, 8)] + [self.tp_peer(j) for j in range(1, 8)]
        for peer in peers + [self.neighbour("z", 1), self.neighbour("z", -1)]:
            pl.semaphore_signal(barrier, inc=1, device_id=peer, device_id_type=pl.DeviceIdType.MESH)
        pl.semaphore_wait(barrier, 16)


def part(buf, lead, sel, rows, cols):
    z = sel.get("z")
    if z is None:
        index = [slice(None), slice(None)]
    elif isinstance(z, int):
        index = [z // 2, z % 2]
    else:
        index = [lax.div(z, 2), lax.rem(z, 2)]
    index += [sel.get(axis, slice(None)) for axis in "yx"]
    return buf.at[tuple(lead) + tuple(index) + (pl.ds(*rows), pl.ds(*cols))]


def send(src, dst, send_sem, recv_sem, device):
    copy = pltpu.make_async_remote_copy(
        src_ref=src, dst_ref=dst, send_sem=send_sem, recv_sem=recv_sem, device_id=device, device_id_type=pl.DeviceIdType.MESH
    )
    copy.start()
    return copy


def arrive(dst, sem, place):
    pltpu.make_async_remote_copy(
        src_ref=dst, dst_ref=dst, send_sem=sem, recv_sem=sem, device_id=place.sibling(), device_id_type=pl.DeviceIdType.MESH
    ).wait_recv()


def gather(place, h, buf, sems, pending):
    send_sems, recv_sems, give_sems, take_sems = sems
    mine, other = (place.core, h), (1 - place.core, h)

    def sel_of(order, k, v):
        return {order[k]: v, **{axis: place.at[axis] for axis in order[k + 1 :]}}

    def give(j):
        for rows, cols, order in ROUTES:
            ref = part(buf, mine, sel_of(order, 2, place.beside(order[2], -j)), rows, cols)
            send(ref, ref, give_sems.at[h], take_sems.at[h], place.sibling())

    one_ring = [buf.at[mine + (0,) * (4 - k)] for k in (0, 1, 2)]
    three_rings = [buf.at[mine + (0, 0, 0, pl.ds(0, 3))], buf.at[mine + (0, 0, pl.ds(0, 3))], buf.at[mine + (slice(None), slice(None), pl.ds(0, 3))]]
    for k in range(3):
        for j in range(1, RING):
            for rows, cols, order in ROUTES:
                ref = part(buf, mine, sel_of(order, k, place.at[order[k]]), rows, cols)
                send(ref, ref, send_sems.at[h, k], recv_sems.at[h, k, j], place.neighbour(order[k], j))
        pending.append((three_rings[k], send_sems.at[h, k]))
        if k == 2:
            give(0)
        yield
        for j in range(1, RING):
            arrive(one_ring[k], recv_sems.at[h, k, j], place)
            if k == 2:
                give(j)
    pending.append((buf.at[mine], give_sems.at[h]))
    yield
    arrive(buf.at[other], take_sems.at[h], place)


def spread(sel, i):
    at, rest = {}, i
    for axis in "xyz":
        if sel.get(axis) is None:
            at[axis] = lax.rem(rest, RING)
            rest = lax.div(rest, RING)
        else:
            at[axis] = sel[axis]
    z = at["z"]
    zh, zl = (z // 2, z % 2) if isinstance(z, int) else (lax.div(z, 2), lax.rem(z, 2))
    return zh, zl, at["y"], at["x"]


def scatter_sum(place, h, sums, landing, result, sems, pending):
    send_sems, recv_sems = sems

    def sel_of(order, k, v, done):
        return {order[k]: v, **{axis: place.at[axis] if done is None else done for axis in order[:k]}}

    def add(order, k, rows, cols):
        window = (pl.ds(*rows), pl.ds(*cols))

        def step(i, carry):
            own = (h,) + spread(sel_of(order, k, place.at[order[k]], None), i) + window
            total = sums[own].astype(jnp.float32)
            for j in range(1, RING):
                total = total + landing[(h,) + spread(sel_of(order, k, j, 0), i) + window].astype(jnp.float32)
            if k == 2:
                result[(h,) + window] = total
            else:
                sums[own] = total.astype(jnp.bfloat16)
            return carry

        lax.fori_loop(0, RING ** (2 - k), step, 0)

    three_rings = [landing.at[h, :, :, pl.ds(0, 3)], landing.at[h, 0, 0, pl.ds(0, 3)], landing.at[h, 0, 0, 0, pl.ds(0, 3)]]
    for k in range(3):
        for j in range(1, RING):
            for rows, cols, order in ROUTES:
                src = part(sums, (h,), sel_of(order, k, place.beside(order[k], j), None), rows, cols)
                dst = part(landing, (h,), sel_of(order, k, j, 0), rows, cols)
                send(src, dst, send_sems.at[h, k], recv_sems.at[h, k], place.neighbour(order[k], j))
        pending.append((three_rings[k], send_sems.at[h, k]))
        yield
        arrive(three_rings[k], recv_sems.at[h, k], place)
        for rows, cols, order in ROUTES:
            add(order, k, rows, cols)


def gelu_pair(pre_act):
    normal_cdf = 0.5 * (1.0 + lax.erf(pre_act * 0.7071067811865476))
    density = jnp.exp(-0.5 * pre_act * pre_act) * 0.3989422804014327
    return (pre_act * normal_cdf, normal_cdf + pre_act * density)


def nt(a, b):
    return lax.dot_general(a, b, (((1,), (1,)), ((), ())), preferred_element_type=jnp.float32)


def nn(a, b):
    return lax.dot_general(a, b, (((1,), (0,)), ((), ())), preferred_element_type=jnp.float32)


def chunk_of(k):
    mm, x, c = lax.div(k, 8), lax.rem(lax.div(k, 2), RING), lax.rem(k, 2)
    return mm, x, c, pl.ds(pl.multiple_of((x * 2 + c) * BLOCK, BLOCK), BLOCK)


def token_rows(buf, h, mm, x, c):
    return buf[c, h, :, mm, :, x].reshape(HALF_TOKENS, BLOCK)


def doc_layout(lengths, token_index):
    doc, start, end = jnp.zeros_like(token_index), jnp.zeros_like(token_index), 0
    for i in range(4):
        end = end + lengths[i]
        passed = (token_index >= end).astype(jnp.int32)
        doc, start = doc + passed, start + passed * lengths[i]
    return doc, token_index - start


def attend_layer(place, refs, bufs, sems, work):
    res, gain, w_query, w_key, w_value, w_output, lengths, freq = refs
    nsend, moved, raw, pair_out, pair_in, own_sum, qkv_out, qkv_in, kv, mixed, part_f, part_out, part_in = bufs
    moved_s, moved_r, raw_s, raw_r, pair_s, pair_r, qkv_s, qkv_r, kv_s, kv_r, mixed_s, mixed_r, part_s, part_r = sems
    dp, tp, core, x = place.dp, place.tp, place.core, place.at["x"]
    pending = []

    for r in range(0, TOK_DEV, 16):
        wide = res[r : r + 16, :].astype(jnp.float32)
        scale = lax.rsqrt(jnp.mean(wide * wide, -1, keepdims=True) + 1e-05)
        normed = (wide * scale * gain[...].astype(jnp.float32)).astype(jnp.bfloat16)
        for d in range(8):
            nsend[d, r : r + 16, :] = normed[:, d * BLOCK : (d + 1) * BLOCK]
    place.enter()
    for j in range(1, 8):
        there = lax.rem(dp + j, 8)
        send(nsend.at[there], moved.at[core, x], moved_s, moved_r, place.dp_peer(j))
    pending.append((nsend.at[pl.ds(0, 7)], moved_s))
    moved[core, x] = nsend[dp]

    def columns(d):
        return pl.ds(pl.multiple_of(d * BLOCK, BLOCK), BLOCK)

    @pl.when(dp == tp)
    def _():
        for j in range(1, 8):
            send(res.at[:, columns(lax.rem(dp + j, 8))], raw, raw_s.at[j], raw_r, place.dp_peer(j))
        raw[...] = res[:, columns(dp)]

    here = dp * TOK_DEV + lax.broadcasted_iota(jnp.int32, (TOK_DEV, 1), 0)
    keys_at = lax.broadcasted_iota(jnp.int32, (1, TOKENS), 1)
    doc, pos = doc_layout(lengths, here)
    key_doc, _ = doc_layout(lengths, keys_at)
    angles = pos.astype(jnp.float32) * freq[...]
    lane = lax.broadcasted_iota(jnp.int32, (1, HEAD_DIM), 1)
    cosine = jnp.cos(angles)
    sine = jnp.sin(angles) * jnp.where(lane < HEAD_DIM // 2, -1.0, 1.0)
    allowed = (doc == key_doc) & (keys_at <= here)
    work(2)

    arrive(nsend.at[pl.ds(0, 7)], moved_r, place)

    def project(c, out):
        rows_in = moved[c].reshape(RING * TOK_DEV, BLOCK)
        for w_ref, at, width in ((w_query, 0, 512), (w_key, 512, 128), (w_value, 640, 128)):
            out[:, :, at : at + width] = nn(rows_in, w_ref[...]).reshape(RING, TOK_DEV, width)

    project(1 - core, pair_out)
    pair = send(pair_out, pair_in, pair_s, pair_r, place.sibling())
    project(core, own_sum)
    pair.wait_recv()
    own_sum[...] = own_sum[...] + pair_in[...]
    qkv_out[...] = own_sum[...].astype(jnp.bfloat16)
    for j in range(1, RING):
        there = lax.rem(x + j, RING)
        send(qkv_out.at[there], qkv_in.at[j], qkv_s, qkv_r, place.dp_peer(2 * j))
    pending.append((qkv_out.at[pl.ds(1, 3)], qkv_s))
    work(2)
    summed = own_sum[x]
    arrive(qkv_in.at[pl.ds(1, 3)], qkv_r, place)
    for j in range(1, RING):
        summed = summed + qkv_in[j].astype(jnp.float32)

    def rotate(values):
        return (values * cosine + pltpu.roll(values, HEAD_DIM // 2, 1) * sine).astype(jnp.bfloat16)

    kv[dp, :, :HEAD_DIM] = rotate(summed[:, 512:640])
    kv[dp, :, HEAD_DIM:] = summed[:, 640:].astype(jnp.bfloat16)
    for j in range(1, 8):
        send(kv.at[dp], kv.at[dp], kv_s, kv_r, place.dp_peer(j))
    pending.append((kv.at[pl.ds(0, 7)], kv_s))
    query = jnp.concatenate([rotate(summed[:, h * HEAD_DIM : (h + 1) * HEAD_DIM]) for h in range(4)], 0)
    work(1)
    arrive(kv.at[pl.ds(0, 7)], kv_r, place)

    all_kv = kv[...].reshape(TOKENS, 2 * HEAD_DIM)
    scores = nt(query, all_kv[:, :HEAD_DIM]) * HEAD_DIM ** (-0.5)
    mask = jnp.concatenate([allowed] * 4, 0)
    terms = jnp.where(mask, jnp.exp(jnp.where(mask, scores, 0.0)), 0.0)
    weights = (terms / jnp.sum(terms, -1, keepdims=True)).astype(jnp.bfloat16)
    heads = nn(weights, all_kv[:, HEAD_DIM:]).astype(jnp.bfloat16)
    for h in range(4):
        mixed[dp, :, h * HEAD_DIM : (h + 1) * HEAD_DIM] = heads[h * TOK_DEV : (h + 1) * TOK_DEV]
    for j in range(1, 8):
        send(mixed.at[dp], mixed.at[dp], mixed_s, mixed_r.at[j], place.dp_peer(j))
    pending.append((mixed.at[pl.ds(0, 7)], mixed_s))

    for j in range(8):
        if j == 1:
            work(2)
        there = lax.rem(dp + 8 - j, 8)
        if j:
            arrive(mixed.at[there], mixed_r.at[j], place)
        out = nn(mixed[there], w_output[...])

        @pl.when(there == tp)
        def _():
            part_f[...] = out

        @pl.when(there != tp)
        def _():
            part_out[there] = out.astype(jnp.bfloat16)
            send(part_out.at[there], part_in.at[tp], part_s, part_r, (place.m, there, dp))

    pending.append((part_out.at[pl.ds(0, 7)], part_s))
    work(1)

    @pl.when(dp != tp)
    def _():
        arrive(raw, raw_r, place)

    total = part_f[...]
    arrive(part_in.at[pl.ds(0, 7)], part_r, place)
    for j in range(1, 8):
        total = total + part_in[lax.rem(tp + j, 8)].astype(jnp.float32)

    @pl.when(dp == tp)
    def _():
        for j in range(1, 8):
            pltpu.make_async_remote_copy(
                src_ref=res.at[:, columns(lax.rem(dp + j, 8))], dst_ref=raw, send_sem=raw_s.at[j], recv_sem=raw_r,
                device_id=place.dp_peer(j), device_id_type=pl.DeviceIdType.MESH,
            ).wait_send()

    pair.wait_send()
    for ref, sem in pending:
        arrive(ref, sem, place)
    return (raw[...].astype(jnp.float32) + total).astype(jnp.bfloat16)


def column_of(row):
    return jnp.broadcast_to(row, (128, 128)).T[:, :1]


def row_of(column):
    return jnp.broadcast_to(column, (128, 128)).T[:1]


SPLIT = 64
ORDER = "a1 n a1 n a1 b1 n b1 n a1 b1 a6 b5 a1 b2 a2 b1 a1 b1 a1 b2 a1 b1 a2 b3"


def step_kernel(
    res, gain, w_query, w_key, w_value, w_output, lengths, freq, w_hbm, enc_ref, dec_ref,
    rows_hbm, errs_hbm, w_out, act_t, pre_t, scale_ref, genc_ref,
    nsend, moved, raw, pair_out, pair_in, own_sum, qkv_out, qkv_in, kv, mixed, part_f, part_out, part_in,
    own_ref, rows, errs, w_raw, w, sums, give, taken, landing, result, total, act, slope, norms, latsum, gsum,
    moved_s, moved_r, raw_s, raw_r, pair_s, pair_r, qkv_s, qkv_r, kv_s, kv_r, mixed_s, mixed_r, part_s, part_r,
    w_sem, rows_send, rows_recv, rows_give, rows_take, errs_send, errs_recv, errs_give, errs_take,
    sum_send, sum_recv, pair_send, pair_recv, out_sem,
):
    place = Place()
    m, core = place.m, place.core
    loads = [
        pltpu.make_async_copy(w_hbm.at[pl.ds(i * SPLIT, SPLIT)], w_raw.at[i % 2], w_sem.at[i % 2])
        for i in range(BLOCK // SPLIT)
    ]
    loads[0].start()
    loads[1].start()
    done = [0]

    def work(count):
        for i in range(done[0], done[0] + count):
            at = pl.ds(i * SPLIT, SPLIT)
            loads[i].wait()

            def step(k, carry):
                cols = pl.ds(pl.multiple_of(k * BLOCK, BLOCK), BLOCK)
                for mm in (0, 1):
                    w[mm, at, cols] = w_raw[i % 2, :, mm, cols]
                return carry

            lax.fori_loop(0, 8, step, 0)
            if i + 2 < len(loads):
                loads[i + 2].start()
        done[0] += count

    layer_bufs = (nsend, moved, raw, pair_out, pair_in, own_sum, qkv_out, qkv_in, kv, mixed, part_f, part_out, part_in)
    layer_sems = (moved_s, moved_r, raw_s, raw_r, pair_s, pair_r, qkv_s, qkv_r, kv_s, kv_r, mixed_s, mixed_r, part_s, part_r)
    layer_refs = (res, gain, w_query, w_key, w_value, w_output, lengths, freq)
    own_ref[...] = attend_layer(place, layer_refs, layer_bufs, layer_sems, work)
    outs = [pltpu.make_async_copy(w, w_out, out_sem.at[4])]
    outs[0].start()
    own = (lax.div(place.at["z"], 2), m, place.at["y"], place.at["x"])
    for h in (0, 1):
        rows[(core, h) + own] = own_ref[h * HALF : (h + 1) * HALF, :]
    rows_sems = (rows_send, rows_recv, rows_give, rows_take)
    errs_sems = (errs_send, errs_recv, errs_give, errs_take)
    pending = []

    def norm_rows(first, count):
        def step(i, carry):
            at = pl.ds(pl.multiple_of(i * 16, 16), 16)
            for mm in (0, 1):
                wide = w[mm, at, :].astype(jnp.float32)
                norms[mm, at, :] = jnp.sqrt(jnp.sum(wide * wide, -1, keepdims=True) + 1e-06)
            return carry

        lax.fori_loop(first, first + count, step, 0)

    def contract(h, buf, first, count):
        if first == 0:
            total[h] = jnp.zeros((BLOCK, HALF_TOKENS), jnp.float32)

        def step(k, carry):
            mm, x, c, cols = chunk_of(k)
            total[h] += nt(w[mm, :, cols], token_rows(buf, h, mm, x, c))
            return carry

        lax.fori_loop(first, first + count, step, 0)

    def decode(h, mm, x, c):
        cols = pl.ds(pl.multiple_of((x * 2 + c) * BLOCK, BLOCK), BLOCK)
        return nn(act[h], w[mm, :, cols])

    blocked = (2, RING, HALF, BLOCK)

    def half_step(h):
        tokens = pl.ds(h * HALF_TOKENS, HALF_TOKENS)
        yield from gather(place, h, rows, rows_sems, pending)
        outs.append(pltpu.make_async_copy(rows.at[:, h], rows_hbm.at[:, h], out_sem.at[h]))
        outs[-1].start()
        contract(h, rows, 0, 8)
        yield
        contract(h, rows, 8, 8)
        for i in range(4):
            at = pl.ds(i * 128, 128)
            lat, slope[h, at, :] = gelu_pair(total[h, at, :] + column_of(enc_ref[i : i + 1, :]))
            latsum[h, at, :] = jnp.sum(lat, -1, keepdims=True)
            act_t[at, tokens] = lat.astype(jnp.bfloat16)
            act[h, :, at] = lat.T.astype(jnp.bfloat16)
        yield
        pairs = []
        for k in range(8):
            mm, x = k // 4, k % 4
            give[h, :, mm, :, x] = decode(h, mm, x, 1 - core).astype(jnp.bfloat16).reshape(blocked)
            ref = (h, slice(None), mm, slice(None), x)
            pairs.append(send(give.at[ref], taken.at[ref], pair_send.at[h, k], pair_recv.at[h, k], place.sibling()))
            if k % 4 == 3:
                yield
        for k in range(8):
            mm, x = k // 4, k % 4
            here = decode(h, mm, x, core)
            pairs[k].wait_recv()
            there = taken[h, :, mm, :, x].reshape(HALF_TOKENS, BLOCK).astype(jnp.float32)
            sums[h, :, mm, :, x] = (here + there).astype(jnp.bfloat16).reshape(blocked)
            if k == 3:
                yield
        pending.extend((give.at[h, :, 0, :, 0], pair_send.at[h, k]) for k in range(8))
        yield from scatter_sum(place, h, sums, landing, result, (sum_send, sum_recv), pending)
        bias = dec_ref[pl.ds(m * 8 + place.dp, 1), :]
        target = own_ref[h * HALF : (h + 1) * HALF, :].astype(jnp.float32)
        errs[(core, h) + own] = (result[h] + bias - target).astype(jnp.bfloat16)
        yield from gather(place, h, errs, errs_sems, pending)
        outs.append(pltpu.make_async_copy(errs.at[:, h], errs_hbm.at[:, h], out_sem.at[2 + h]))
        outs[-1].start()
        contract(h, errs, 0, 8)
        yield
        contract(h, errs, 8, 8)
        for i in range(4):
            at = pl.ds(i * 128, 128)
            norm_total = norms[0, at, :] + norms[1, at, :]
            pre_grad = (2.0 / TOKENS * total[h, at, :] + sparsity / TOKENS * norm_total) * slope[h, at, :]
            gsum[h, at, :] = jnp.sum(pre_grad, -1, keepdims=True)
            pre_t[at, tokens] = pre_grad.astype(jnp.bfloat16)

    halves = {"a": half_step(0), "b": half_step(1)}
    normed = 0
    for turn in ORDER.split():
        if turn == "n":
            norm_rows(8 * normed, 8)
            normed += 1
        else:
            for _ in range(int(turn[1:])):
                next(halves[turn[0]], None)
    for i in range(4):
        at = pl.ds(i * 128, 128)
        genc_ref[i : i + 1, :] = row_of(gsum[0, at, :] + gsum[1, at, :])
    scale_ref[...] = sparsity / TOKENS * (latsum[0] + latsum[1]) / norms[...]
    for copy in outs:
        copy.wait()
    for ref, sem in pending:
        arrive(ref, sem, place)


def grad_kernel(rows, errs, w, act_t, pre_t, scale, genc, gw, genc_out, gdec):
    for mm in (0, 1):
        err = errs[0, :, :, mm, :, 0].reshape(TOKENS, BLOCK)
        grad = 2.0 / TOKENS * nn(act_t[...], err) + nn(pre_t[...], rows[0, :, :, mm, :, 0].reshape(TOKENS, BLOCK))
        gw[:, mm, :] = (grad + scale[mm] * w[mm].astype(jnp.float32)).astype(jnp.bfloat16)
        ones = jnp.ones((16, TOKENS), jnp.bfloat16)
        gdec[mm : mm + 1, :] = 2.0 / TOKENS * nn(ones, err)[:1]
    genc_out[...] = genc[...]


def shards(
    residual, norm_gain, w_query, w_key, w_value, w_output, doc_lengths, coder_weight, enc_bias, dec_bias
):
    latents, _, features = coder_weight.shape
    blocks = (2, 2, 2, RING, RING, HALF, BLOCK)
    bf16, f32 = jnp.bfloat16, jnp.float32
    dma, vm = pltpu.SemaphoreType.DMA, pltpu.VMEM
    vmem = pl.BlockSpec(memory_space=pltpu.VMEM)
    hbm = pl.BlockSpec(memory_space=pl.ANY)
    ring = [dma((2, 3)), dma((2, 3, RING)), dma((2,)), dma((2,))]
    half = np.arange(HEAD_DIM // 2)
    freq = np.concatenate([rope_base ** (-half * 2.0 / HEAD_DIM)] * 2)[None].astype(np.float32)
    block = (TOK_DEV, BLOCK)
    rows, errs, w_t, act_t, pre_t, scale, genc = pl.pallas_call(
        step_kernel,
        out_shape=(
            jax.ShapeDtypeStruct((2,) + blocks, bf16),
            jax.ShapeDtypeStruct((2,) + blocks, bf16),
            jax.ShapeDtypeStruct((2, latents, features), bf16),
            jax.ShapeDtypeStruct((latents, TOKENS), bf16),
            jax.ShapeDtypeStruct((latents, TOKENS), bf16),
            jax.ShapeDtypeStruct((2, latents, 1), f32),
            jax.ShapeDtypeStruct((4, 128), f32),
        ),
        in_specs=[vmem] * 6 + [pl.BlockSpec(memory_space=pltpu.SMEM), vmem, hbm, vmem, vmem],
        out_specs=(hbm, hbm, hbm, vmem, vmem, vmem, vmem),
        scratch_shapes=[
            vm((8,) + block, bf16),
            vm((2, RING) + block, bf16),
            vm(block, bf16),
            vm((RING, TOK_DEV, 768), f32),
            vm((RING, TOK_DEV, 768), f32),
            vm((RING, TOK_DEV, 768), f32),
            vm((RING, TOK_DEV, 768), bf16),
            vm((RING, TOK_DEV, 768), bf16),
            vm((8, TOK_DEV, 2 * HEAD_DIM), bf16),
            vm((8,) + block, bf16),
            vm(block, f32),
            vm((8,) + block, bf16),
            vm((8,) + block, bf16),
            vm(block, bf16),
            vm((2,) + blocks, bf16),
            vm((2,) + blocks, bf16),
            vm((2, SPLIT, 2, features), bf16),
            vm((2, latents, features), bf16),
            vm(blocks, bf16),
            vm(blocks, bf16),
            vm(blocks, bf16),
            vm(blocks, bf16),
            vm((2, HALF, BLOCK), f32),
            vm((2, latents, HALF_TOKENS), f32),
            vm((2, HALF_TOKENS, latents), bf16),
            vm((2, latents, HALF_TOKENS), f32),
            vm((2, latents, 1), f32),
            vm((2, latents, 1), f32),
            vm((2, latents, 1), f32),
            *[dma(()), dma(()), dma((8,)), dma(()), dma(()), dma(())],
            *[dma(()), dma(()), dma(()), dma(()), dma(()), dma((8,)), dma(()), dma(())],
            dma((2,)),
            *ring,
            *ring,
            dma((2, 3)),
            dma((2, 3)),
            dma((2, 8)),
            dma((2, 8)),
            dma((5,)),
        ],
        compiler_params=pltpu.CompilerParams(collective_id=0, has_side_effects=True, vmem_limit_bytes=62 * 1024 * 1024),
        cost_estimate=pl.CostEstimate(flops=6 * TOKENS * latents * 2 * features, bytes_accessed=40 << 20, transcendentals=0),
    )(
        residual[0], norm_gain, w_query[0], w_key[0], w_value[0], w_output[0], doc_lengths, jnp.asarray(freq),
        coder_weight, enc_bias.reshape(4, 128), dec_bias.reshape(16, BLOCK),
    )
    set_spec = pl.BlockSpec(
        (1, 2, 2, 2, RING, 1, HALF, BLOCK), lambda k: (lax.rem(k, 2), 0, 0, 0, 0, lax.div(k, 2), 0, 0)
    )
    whole = lambda *shape: pl.BlockSpec(shape, lambda k: (0,) * len(shape))
    weight_grad, grad_enc, grad_dec = pl.pallas_call(
        grad_kernel,
        grid=(8,),
        out_shape=(
            jax.ShapeDtypeStruct((latents, 2, features), bf16),
            jax.ShapeDtypeStruct((4, 128), f32),
            jax.ShapeDtypeStruct((2, features), f32),
        ),
        in_specs=[
            set_spec,
            set_spec,
            pl.BlockSpec((2, latents, BLOCK), lambda k: (0, 0, k)),
            whole(latents, TOKENS),
            whole(latents, TOKENS),
            whole(2, latents, 1),
            whole(4, 128),
        ],
        out_specs=(
            pl.BlockSpec((latents, 2, BLOCK), lambda k: (0, 0, k)),
            whole(4, 128),
            pl.BlockSpec((2, BLOCK), lambda k: (0, k)),
        ),
        compiler_params=pltpu.CompilerParams(vmem_limit_bytes=62 * 1024 * 1024),
    )(rows, errs, w_t, act_t, pre_t, scale, genc)
    return (weight_grad, grad_enc.reshape(-1), grad_dec)


def solution(mesh):
    return jax.shard_map(
        shards,
        mesh=mesh,
        in_specs=(
            P("grp", "dp", None),
            P("grp", None),
            P("grp", "dp", "tp"),
            P("grp", "dp", "tp"),
            P("grp", "dp", "tp"),
            P("grp", "tp", "dp"),
            P(),
            P(("grp", "tp", "dp"), None, None),
            P(("grp", "tp", "dp")),
            P(),
        ),
        out_specs=(P(("grp", "tp", "dp"), None, None), P(("grp", "tp", "dp")), P()),
        check_vma=False,
    )
```

time: 209 us -> 176 us (0.84)
  Pallas kernels: 203 us -> 174 us
  local copies, waits for them, and re-layouts: 5.14 us -> 1.4 us
    pallas_call x1, Pallas kernels: 184 us -> 154 us  [shards(): pl.pallas_call(step_kernel, out_shape=(jax.ShapeDtypeStruct((2,) + blocks...]
    unnamed x8 -> x0, local copies, waits for them, and re-layouts: 3.74 us -> none
where the time goes in v3:
time: 176 us
  Pallas kernels  174 us (99%)
    pallas_call x1, Pallas kernels, shards(): pl.pallas_call(step_kernel, out_shape=(jax.ShapeDtypeStruct((2,) + blocks...  154 us
    pallas_call x1, Pallas kernels, shards(): pl.pallas_call(grad_kernel, grid=(8,), out_shape=(jax.ShapeDtypeStruct((l...  19.7 us

profile of v3, /device:TPU:1, one launch (start us, length us, event | category | flops | bytes accessed | tf_op | source)
XLA Modules:
  0.0 176.2 jit_solution(18123190268953844576)
XLA Ops:
  0.6 1.4 reshape.16.dec_ref
  2.0 154.4 %shard_map.130 = (bf16[2,2,2,2,4,4,32,512]{7,6,5,4,3,2,1,0:T(8,128)(2,1)}, bf16[2,2,2,2,4,4,32,512]{7,6,5,4,3,2,1,0:T(8,128)(2,1)}, bf16[2,512,4096]{2,1,0:T(8,1...) custom-call(bf16[64,4096]{1,0:T(8,128)(2,1)} %bitcast.7, ...), custom_call_target="tpu_custom_call" | custom-call | flops 12884901888 | bytes 41943040 | tf_op jit(solution)/shard_map/pallas_call | solution.py:506
  156.5 19.7 %shard_map.131 = (bf16[512,2,4096]{2,1,0:T(2,128)(2,1)}, f32[4,128]{1,0:T(4,128)}, f32[2,4096]{1,0:T(2,128)}) custom-call(bf16[2,2,2,2,4,4,32,512]{7,6,5,4,3,2,1,0:T(8,128)(2,1)} %get-tuple-element.13.rows, bf16[2,2,2,2,4,4,32,512]{7,6,5,4,3,2,1,0:T(8,128)(2,1)} %get-tuple-element.14.errs, bf16[2,512,4096]{2,1,0:T(8,128)(2,1)} %get-tuple-element.15.w, ...), custom_call_target="tpu_custom_call" | custom-call | tf_op jit(solution)/shard_map/pallas_call | solution.py:570

commit v4 on v3

--- a/solution.py
+++ b/solution.py
@@ -84,7 +84,7 @@
 
 def gather(place, h, buf, sems, pending):
     send_sems, recv_sems, give_sems, take_sems = sems
-    mine, other = (place.core, h), (1 - place.core, h)
+    mine = (place.core, h)
 
     def sel_of(order, k, v):
         return {order[k]: v, **{axis: place.at[axis] for axis in order[k + 1 :]}}
@@ -97,7 +97,7 @@
     one_ring = [buf.at[mine + (0,) * (4 - k)] for k in (0, 1, 2)]
     three_rings = [buf.at[mine + (0, 0, 0, pl.ds(0, 3))], buf.at[mine + (0, 0, pl.ds(0, 3))], buf.at[mine + (slice(None), slice(None), pl.ds(0, 3))]]
     for k in range(3):
-        for j in range(1, RING):
+        for j in (2, 1, 3):
             for rows, cols, order in ROUTES:
                 ref = part(buf, mine, sel_of(order, k, place.at[order[k]]), rows, cols)
                 send(ref, ref, send_sems.at[h, k], recv_sems.at[h, k, j], place.neighbour(order[k], j))
@@ -105,13 +105,11 @@
         if k == 2:
             give(0)
         yield
-        for j in range(1, RING):
+        for j in (1, 3, 2):
             arrive(one_ring[k], recv_sems.at[h, k, j], place)
             if k == 2:
                 give(j)
     pending.append((buf.at[mine], give_sems.at[h]))
-    yield
-    arrive(buf.at[other], take_sems.at[h], place)
 
 
 def spread(sel, i):
@@ -151,7 +149,7 @@
 
     three_rings = [landing.at[h, :, :, pl.ds(0, 3)], landing.at[h, 0, 0, pl.ds(0, 3)], landing.at[h, 0, 0, 0, pl.ds(0, 3)]]
     for k in range(3):
-        for j in range(1, RING):
+        for j in (2, 1, 3):
             for rows, cols, order in ROUTES:
                 src = part(sums, (h,), sel_of(order, k, place.beside(order[k], j), None), rows, cols)
                 dst = part(landing, (h,), sel_of(order, k, j, 0), rows, cols)
@@ -175,11 +173,6 @@
 
 def nn(a, b):
     return lax.dot_general(a, b, (((1,), (0,)), ((), ())), preferred_element_type=jnp.float32)
-
-
-def chunk_of(k):
-    mm, x, c = lax.div(k, 8), lax.rem(lax.div(k, 2), RING), lax.rem(k, 2)
-    return mm, x, c, pl.ds(pl.multiple_of((x * 2 + c) * BLOCK, BLOCK), BLOCK)
 
 
 def token_rows(buf, h, mm, x, c):
@@ -334,7 +327,7 @@
 
 
 SPLIT = 64
-ORDER = "a1 n a1 n a1 b1 n b1 n a1 b1 a6 b5 a1 b2 a2 b1 a1 b1 a1 b2 a1 b1 a2 b3"
+ORDER = "a1 n a1 b1 n a1 b1 b1 n a1 a5 b1 n b3 a1 b2 a2 b1 a1 b1 a1 b3 a2 b2"
 
 
 def step_kernel(
@@ -395,16 +388,26 @@
 
         lax.fori_loop(first, first + count, step, 0)
 
-    def contract(h, buf, first, count):
-        if first == 0:
+    def contract(h, buf, c, fresh):
+        if fresh:
             total[h] = jnp.zeros((BLOCK, HALF_TOKENS), jnp.float32)
 
         def step(k, carry):
-            mm, x, c, cols = chunk_of(k)
+            mm, x = lax.div(k, RING), lax.rem(k, RING)
+            cols = pl.ds(pl.multiple_of((x * 2 + c) * BLOCK, BLOCK), BLOCK)
             total[h] += nt(w[mm, :, cols], token_rows(buf, h, mm, x, c))
             return carry
 
-        lax.fori_loop(first, first + count, step, 0)
+        lax.fori_loop(0, 2 * RING, step, 0)
+
+    def contract_all(h, buf, take_sems, first_out):
+        contract(h, buf, core, True)
+        yield
+        arrive(buf.at[1 - core, h], take_sems.at[h], place)
+        out_hbm = (rows_hbm, errs_hbm)[first_out // 2]
+        outs.append(pltpu.make_async_copy(buf.at[:, h], out_hbm.at[:, h], out_sem.at[first_out + h]))
+        outs[-1].start()
+        contract(h, buf, 1 - core, False)
 
     def decode(h, mm, x, c):
         cols = pl.ds(pl.multiple_of((x * 2 + c) * BLOCK, BLOCK), BLOCK)
@@ -415,11 +418,7 @@
     def half_step(h):
         tokens = pl.ds(h * HALF_TOKENS, HALF_TOKENS)
         yield from gather(place, h, rows, rows_sems, pending)
-        outs.append(pltpu.make_async_copy(rows.at[:, h], rows_hbm.at[:, h], out_sem.at[h]))
-        outs[-1].start()
-        contract(h, rows, 0, 8)
-        yield
-        contract(h, rows, 8, 8)
+        yield from contract_all(h, rows, rows_take, 0)
         for i in range(4):
             at = pl.ds(i * 128, 128)
             lat, slope[h, at, :] = gelu_pair(total[h, at, :] + column_of(enc_ref[i : i + 1, :]))
@@ -445,15 +444,11 @@
                 yield
         pending.extend((give.at[h, :, 0, :, 0], pair_send.at[h, k]) for k in range(8))
         yield from scatter_sum(place, h, sums, landing, result, (sum_send, sum_recv), pending)
-        bias = dec_ref[pl.ds(m * 8 + place.dp, 1), :]
+        bias = dec_ref[pl.ds(m, 1), pl.ds(pl.multiple_of(place.dp * BLOCK, BLOCK), BLOCK)]
         target = own_ref[h * HALF : (h + 1) * HALF, :].astype(jnp.float32)
         errs[(core, h) + own] = (result[h] + bias - target).astype(jnp.bfloat16)
         yield from gather(place, h, errs, errs_sems, pending)
-        outs.append(pltpu.make_async_copy(errs.at[:, h], errs_hbm.at[:, h], out_sem.at[2 + h]))
-        outs[-1].start()
-        contract(h, errs, 0, 8)
-        yield
-        contract(h, errs, 8, 8)
+        yield from contract_all(h, errs, errs_take, 2)
         for i in range(4):
             at = pl.ds(i * 128, 128)
             norm_total = norms[0, at, :] + norms[1, at, :]
@@ -561,7 +556,7 @@
         cost_estimate=pl.CostEstimate(flops=6 * TOKENS * latents * 2 * features, bytes_accessed=40 << 20, transcendentals=0),
     )(
         residual[0], norm_gain, w_query[0], w_key[0], w_value[0], w_output[0], doc_lengths, jnp.asarray(freq),
-        coder_weight, enc_bias.reshape(4, 128), dec_bias.reshape(16, BLOCK),
+        coder_weight, enc_bias.reshape(4, 128), dec_bias,
     )
     set_spec = pl.BlockSpec(
         (1, 2, 2, 2, RING, 1, HALF, BLOCK), lambda k: (lax.rem(k, 2), 0, 0, 0, 0, lax.div(k, 2), 0, 0)

time: 176 us -> 169 us (0.960)
  Pallas kernels: 174 us -> 168 us
    pallas_call x1, Pallas kernels: 154 us -> 148 us  [shards(): pl.pallas_call(step_kernel, out_shape=(jax.ShapeDtypeStruct((2,) + blocks...]
where the time goes in v4:
time: 169 us
  Pallas kernels  168 us (99%)
    pallas_call x1, Pallas kernels, shards(): pl.pallas_call(step_kernel, out_shape=(jax.ShapeDtypeStruct((2,) + blocks...  148 us
    pallas_call x1, Pallas kernels, shards(): pl.pallas_call(grad_kernel, grid=(8,), out_shape=(jax.ShapeDtypeStruct((l...  19.7 us

profile of v4, /device:TPU:1, one launch (start us, length us, event | category | flops | bytes accessed | tf_op | source)
XLA Modules:
  0.0 168.8 jit_solution(510137704487472287)
XLA Ops:
  0.6 148.5 %shard_map.130 = (bf16[2,2,2,2,4,4,32,512]{7,6,5,4,3,2,1,0:T(8,128)(2,1)}, bf16[2,2,2,2,4,4,32,512]{7,6,5,4,3,2,1,0:T(8,128)(2,1)}, bf16[2,512,4096]{2,1,0:T(8,1...) custom-call(bf16[64,4096]{1,0:T(8,128)(2,1)} %bitcast.7, ...), custom_call_target="tpu_custom_call" | custom-call | flops 12884901888 | bytes 41943040 | tf_op jit(solution)/shard_map/pallas_call | solution.py:501
  149.1 19.7 %shard_map.131 = (bf16[512,2,4096]{2,1,0:T(2,128)(2,1)}, f32[4,128]{1,0:T(4,128)}, f32[2,4096]{1,0:T(2,128)}) custom-call(bf16[2,2,2,2,4,4,32,512]{7,6,5,4,3,2,1,0:T(8,128)(2,1)} %get-tuple-element.13.rows, bf16[2,2,2,2,4,4,32,512]{7,6,5,4,3,2,1,0:T(8,128)(2,1)} %get-tuple-element.14.errs, bf16[2,512,4096]{2,1,0:T(8,128)(2,1)} %get-tuple-element.15.w, ...), custom_call_target="tpu_custom_call" | custom-call | tf_op jit(solution)/shard_map/pallas_call | solution.py:565

commit v5 on v4

--- a/solution.py
+++ b/solution.py
@@ -211,12 +211,6 @@
     def columns(d):
         return pl.ds(pl.multiple_of(d * BLOCK, BLOCK), BLOCK)
 
-    @pl.when(dp == tp)
-    def _():
-        for j in range(1, 8):
-            send(res.at[:, columns(lax.rem(dp + j, 8))], raw, raw_s.at[j], raw_r, place.dp_peer(j))
-        raw[...] = res[:, columns(dp)]
-
     here = dp * TOK_DEV + lax.broadcasted_iota(jnp.int32, (TOK_DEV, 1), 0)
     keys_at = lax.broadcasted_iota(jnp.int32, (1, TOKENS), 1)
     doc, pos = doc_layout(lengths, here)
@@ -226,7 +220,7 @@
     cosine = jnp.cos(angles)
     sine = jnp.sin(angles) * jnp.where(lane < HEAD_DIM // 2, -1.0, 1.0)
     allowed = (doc == key_doc) & (keys_at <= here)
-    work(2)
+    work(4)
 
     arrive(nsend.at[pl.ds(0, 7)], moved_r, place)
 
@@ -259,8 +253,15 @@
     for j in range(1, 8):
         send(kv.at[dp], kv.at[dp], kv_s, kv_r, place.dp_peer(j))
     pending.append((kv.at[pl.ds(0, 7)], kv_s))
+
+    @pl.when(dp == tp)
+    def _():
+        for j in range(1, 8):
+            send(res.at[:, columns(lax.rem(dp + j, 8))], raw, raw_s.at[j], raw_r, place.dp_peer(j))
+        raw[...] = res[:, columns(dp)]
+
     query = jnp.concatenate([rotate(summed[:, h * HEAD_DIM : (h + 1) * HEAD_DIM]) for h in range(4)], 0)
-    work(1)
+    work(2)
     arrive(kv.at[pl.ds(0, 7)], kv_r, place)
 
     all_kv = kv[...].reshape(TOKENS, 2 * HEAD_DIM)
@@ -271,16 +272,23 @@
     heads = nn(weights, all_kv[:, HEAD_DIM:]).astype(jnp.bfloat16)
     for h in range(4):
         mixed[dp, :, h * HEAD_DIM : (h + 1) * HEAD_DIM] = heads[h * TOK_DEV : (h + 1) * TOK_DEV]
-    for j in range(1, 8):
+    sibling = dp + 1 - 2 * core
+    send(mixed.at[dp], mixed.at[dp], mixed_s, mixed_r.at[1], place.sibling())
+    for j in (2, 4, 6):
         send(mixed.at[dp], mixed.at[dp], mixed_s, mixed_r.at[j], place.dp_peer(j))
     pending.append((mixed.at[pl.ds(0, 7)], mixed_s))
 
-    for j in range(8):
+    for j in (0, 1, 2, 6, 4, 3, 7, 5):
         if j == 1:
-            work(2)
-        there = lax.rem(dp + 8 - j, 8)
+            there = sibling
+        elif j % 2:
+            there = lax.rem(sibling + 8 - (j - 1), 8)
+        else:
+            there = lax.rem(dp + 8 - j, 8)
         if j:
             arrive(mixed.at[there], mixed_r.at[j], place)
+        if j in (2, 4, 6):
+            send(mixed.at[there], mixed.at[there], mixed_s, mixed_r.at[j + 1], place.sibling())
         out = nn(mixed[there], w_output[...])
 
         @pl.when(there == tp)
@@ -293,7 +301,6 @@
             send(part_out.at[there], part_in.at[tp], part_s, part_r, (place.m, there, dp))
 
     pending.append((part_out.at[pl.ds(0, 7)], part_s))
-    work(1)
 
     @pl.when(dp != tp)
     def _():
@@ -476,12 +483,15 @@
 
 
 def grad_kernel(rows, errs, w, act_t, pre_t, scale, genc, gw, genc_out, gdec):
-    for mm in (0, 1):
-        err = errs[0, :, :, mm, :, 0].reshape(TOKENS, BLOCK)
-        grad = 2.0 / TOKENS * nn(act_t[...], err) + nn(pre_t[...], rows[0, :, :, mm, :, 0].reshape(TOKENS, BLOCK))
-        gw[:, mm, :] = (grad + scale[mm] * w[mm].astype(jnp.float32)).astype(jnp.bfloat16)
-        ones = jnp.ones((16, TOKENS), jnp.bfloat16)
-        gdec[mm : mm + 1, :] = 2.0 / TOKENS * nn(ones, err)[:1]
+    ones = jnp.ones((16, TOKENS), jnp.bfloat16)
+    for c in (0, 1):
+        cols = pl.ds(c * BLOCK, BLOCK)
+        for mm in (0, 1):
+            err = errs[c, :, :, mm, :, 0].reshape(TOKENS, BLOCK)
+            row = rows[c, :, :, mm, :, 0].reshape(TOKENS, BLOCK)
+            grad = 2.0 / TOKENS * nn(act_t[...], err) + nn(pre_t[...], row)
+            gw[:, mm, cols] = (grad + scale[mm] * w[mm, :, cols].astype(jnp.float32)).astype(jnp.bfloat16)
+            gdec[mm : mm + 1, cols] = 2.0 / TOKENS * nn(ones, err)[:1]
     genc_out[...] = genc[...]
 
 
@@ -559,12 +569,12 @@
         coder_weight, enc_bias.reshape(4, 128), dec_bias,
     )
     set_spec = pl.BlockSpec(
-        (1, 2, 2, 2, RING, 1, HALF, BLOCK), lambda k: (lax.rem(k, 2), 0, 0, 0, 0, lax.div(k, 2), 0, 0)
+        (2, 2, 2, 2, RING, 1, HALF, BLOCK), lambda k: (0, 0, 0, 0, 0, k, 0, 0)
     )
     whole = lambda *shape: pl.BlockSpec(shape, lambda k: (0,) * len(shape))
     weight_grad, grad_enc, grad_dec = pl.pallas_call(
         grad_kernel,
-        grid=(8,),
+        grid=(RING,),
         out_shape=(
             jax.ShapeDtypeStruct((latents, 2, features), bf16),
             jax.ShapeDtypeStruct((4, 128), f32),
@@ -573,16 +583,16 @@
         in_specs=[
             set_spec,
             set_spec,
-            pl.BlockSpec((2, latents, BLOCK), lambda k: (0, 0, k)),
+            pl.BlockSpec((2, latents, 2 * BLOCK), lambda k: (0, 0, k)),
             whole(latents, TOKENS),
             whole(latents, TOKENS),
             whole(2, latents, 1),
             whole(4, 128),
         ],
         out_specs=(
-            pl.BlockSpec((latents, 2, BLOCK), lambda k: (0, 0, k)),
+            pl.BlockSpec((latents, 2, 2 * BLOCK), lambda k: (0, 0, k)),
             whole(4, 128),
-            pl.BlockSpec((2, BLOCK), lambda k: (0, k)),
+            pl.BlockSpec((2, 2 * BLOCK), lambda k: (0, k)),
         ),
         compiler_params=pltpu.CompilerParams(vmem_limit_bytes=62 * 1024 * 1024),
     )(rows, errs, w_t, act_t, pre_t, scale, genc)

time: 169 us -> 168 us (level)
  no operation moved by 1% of the time
where the time goes in v5:
time: 168 us
  Pallas kernels  167 us (99%)
    pallas_call x1, Pallas kernels, shards(): pl.pallas_call(step_kernel, out_shape=(jax.ShapeDtypeStruct((2,) + blocks...  148 us
    pallas_call x1, Pallas kernels, shards(): pl.pallas_call(grad_kernel, grid=(RING,), out_shape=(jax.ShapeDtypeStruct...  19.1 us

profile of v5, /device:TPU:1, one launch (start us, length us, event | category | flops | bytes accessed | tf_op | source)
XLA Modules:
  0.0 168.0 jit_solution(13848372005084008215)
XLA Ops:
  0.6 148.2 %shard_map.130 = (bf16[2,2,2,2,4,4,32,512]{7,6,5,4,3,2,1,0:T(8,128)(2,1)}, bf16[2,2,2,2,4,4,32,512]{7,6,5,4,3,2,1,0:T(8,128)(2,1)}, bf16[2,512,4096]{2,1,0:T(8,1...) custom-call(bf16[64,4096]{1,0:T(8,128)(2,1)} %bitcast.7, ...), custom_call_target="tpu_custom_call" | custom-call | flops 12884901888 | bytes 41943040 | tf_op jit(solution)/shard_map/pallas_call | solution.py:511
  148.9 19.1 %shard_map.131 = (bf16[512,2,4096]{2,1,0:T(2,128)(2,1)}, f32[4,128]{1,0:T(4,128)}, f32[2,4096]{1,0:T(2,128)}) custom-call(bf16[2,2,2,2,4,4,32,512]{7,6,5,4,3,2,1,0:T(8,128)(2,1)} %get-tuple-element.13.rows, bf16[2,2,2,2,4,4,32,512]{7,6,5,4,3,2,1,0:T(8,128)(2,1)} %get-tuple-element.14.errs, bf16[2,512,4096]{2,1,0:T(8,128)(2,1)} %get-tuple-element.15.w, ...), custom_call_target="tpu_custom_call" | custom-call | tf_op jit(solution)/shard_map/pallas_call | solution.py:575
